TPU v7x, 32 devices: a whole 2x2x4 slice. The times are simulated.
32 devices in a mesh: groups: 2 (over y), ctx: 4 (over z), exp: 2 (over x), head: 2 (over core).
Axes of the slice: x: 2, y: 2, z: 4, core: 2. Of those that a mesh axis runs over, the one named last changes fastest.
Arguments:
- latent: bfloat16 [256, 576], P(('groups', 'ctx')), parts along dimension 0, may hold values from -5 to 5
- query: bfloat16 [256, 3072], P(('groups', 'ctx'), ('exp', 'head')), parts along dimension 0, may hold values from -30 to 30
- w_uk: bfloat16 [512, 2048], P(None, ('exp', 'head')), may hold values from -0.25 to 0.25
- w_uv: bfloat16 [512, 2048], P(None, ('exp', 'head')), may hold values from -0.25 to 0.25
- w_o: bfloat16 [2048, 3584], P(('exp', 'head'), 'ctx'), may hold values from -0.5 to 0.5
- resid: bfloat16 [256, 3584], P(('groups', 'ctx', 'exp', 'head')), parts along dimension 0, may hold values from -6 to 6
- norm_gain: float32 [3584], replicated, may hold values from 0.1 to 1.9
- w_gate: bfloat16 [4, 3584, 2048], P(('exp', 'head'), None, 'ctx'), may hold values from -0.09375 to 0.09375
- w_up: bfloat16 [4, 3584, 2048], P(('exp', 'head'), None, 'ctx'), may hold values from -0.09375 to 0.09375
- w_down: bfloat16 [4, 2048, 3584], P(('exp', 'head'), None, 'ctx'), may hold values from -0.125 to 0.125
- expert_ids: int32 [256, 2], P(('groups', 'ctx', 'exp', 'head')), parts along dimension 0, may hold values from 0 to 3, all different within a row; in each aligned block of 8 rows (0 to 7, 8 to 15, ...) at most 8 rows name the same one
- route_weights: float32 [256, 2], P(('groups', 'ctx', 'exp', 'head')), parts along dimension 0, may hold values from 0.2 to 1
Outputs:
- layer_out: bfloat16 [256, 3584], P(('groups', 'ctx', 'exp', 'head')), parts along dimension 0
There are 2 independent parts, one for each index of `groups`. A program takes and returns all parts, laid end to end along the dimension named above; an argument that names none is the same for every part. Nothing has to cross between parts.
Inputs may be any that keep to these rules, and one draw needn't show every extreme that they name: `expert_ids`: each token names 2 different experts; within each aligned block of 8 tokens no expert is named more than 8 times, a bound that some block reaches.
All inputs are finite; a program needn't handle non-finite values.
Results may differ from a plain program's by a relative error of at most 0.014.
Values may be sent and summed in bfloat16 or wider, within the bound.
No kernel may reach another device: no remote copies, remote signals or barrier semaphores. Data moves between devices by JAX's collectives and lax.ppermute only.
A program may use at most 64 MiB of HBM per device.

v0:
```python
import math

import jax
import jax.numpy as jnp
from jax import lax
from jax.sharding import PartitionSpec as P

D = 3584
NOPE = 128
ROPE = 64
LATENT = 512


def shards(
    latent,
    query,
    w_uk,
    w_uv,
    w_o,
    resid,
    norm_gain,
    w_gate,
    w_up,
    w_down,
    expert_ids,
    route_weights,
):
    qblock = query.shape[0]
    head_width = NOPE + ROPE
    heads_here = query.shape[1] // head_width
    nope_span = heads_here * NOPE
    score_scale = 1.0 / math.sqrt(head_width)
    query_all = query.reshape(qblock, heads_here, head_width)
    query_nope = query_all[:, :, :NOPE]
    query_rope = query_all[:, :, NOPE:]
    query_pos = lax.axis_index("ctx") * qblock + jnp.arange(qblock, dtype=jnp.int32)
    shard_rows = lax.all_gather(latent, "ctx", axis=0, tiled=True)
    piece_rows = shard_rows.shape[0]
    compressed = shard_rows[:, :LATENT]
    key_nope = (
        jnp.dot(compressed, w_uk, preferred_element_type=jnp.float32)
        .astype(jnp.bfloat16)
        .reshape(piece_rows, heads_here, NOPE)
    )
    values = (
        jnp.dot(compressed, w_uv, preferred_element_type=jnp.float32)
        .astype(jnp.bfloat16)
        .reshape(piece_rows, heads_here, NOPE)
    )
    run_max = jnp.full((qblock, heads_here), -1e30, jnp.float32)
    piece_rows = key_nope.shape[0]
    scores = jnp.einsum("qhd,khd->qhk", query_nope, key_nope, preferred_element_type=jnp.float32)
    scores = (
        scores
        + jnp.einsum(
            "qhd,kd->qhk", query_rope, shard_rows[:, LATENT:], preferred_element_type=jnp.float32
        )
    ) * score_scale
    key_pos = jnp.arange(piece_rows, dtype=jnp.int32)
    allowed = (key_pos[None, :] <= query_pos[:, None])[:, None, :]
    new_max = jnp.maximum(run_max, jnp.max(jnp.where(allowed, scores, -1e30), axis=2))
    exponent = jnp.where(allowed, jnp.exp(scores - new_max[:, :, None]), 0.0)
    run_sum = jnp.sum(exponent, axis=2)
    weighted_sum = jnp.einsum(
        "qhk,khd->qhd", exponent.astype(jnp.bfloat16), values, preferred_element_type=jnp.float32
    )
    attn_state = (new_max, run_sum, weighted_sum)
    run_max, run_sum, weighted_sum = attn_state
    attended = (weighted_sum / run_sum[:, :, None]).astype(jnp.bfloat16).reshape(qblock, nope_span)
    tok_dev = resid.shape[0]
    ctx_count = lax.axis_size("ctx")
    partial_value = jnp.dot(
        lax.all_gather(attended, "ctx", axis=0, tiled=True), w_o, preferred_element_type=jnp.float32
    )
    partial_value = partial_value.astype(jnp.bfloat16).reshape(ctx_count, qblock, w_o.shape[1])
    summed = lax.psum_scatter(
        partial_value, ("exp", "head"), scatter_dimension=1, tiled=True
    ).astype(jnp.float32)
    swapped = lax.all_to_all(
        summed.astype(jnp.bfloat16), "ctx", split_axis=0, concat_axis=2, tiled=True
    ).astype(summed.dtype)
    projected = swapped.reshape(tok_dev, D)
    residual_sum = resid.astype(jnp.float32) + projected
    inverse_rms = lax.rsqrt(jnp.mean(residual_sum * residual_sum, axis=1, keepdims=True) + 1e-06)
    normalized = (residual_sum * inverse_rms * norm_gain).astype(jnp.bfloat16)
    experts = lax.axis_size(("exp", "head"))
    top_count = expert_ids.shape[1]
    capacity = max(2, 2 * tok_dev * top_count // experts)
    flat_ids = expert_ids.reshape(-1)
    onehot = (flat_ids[:, None] == jnp.arange(experts, dtype=jnp.int32)[None, :]).astype(jnp.int32)
    slot_rank = jnp.sum((jnp.cumsum(onehot, axis=0) - onehot) * onehot, axis=1)
    target = (flat_ids * capacity + slot_rank).reshape(tok_dev, top_count)
    slot_ids = jnp.arange(experts * capacity, dtype=jnp.int32)
    route_hits = (target[:, :, None] == slot_ids[None, None, :]).astype(jnp.float32)
    picker = jnp.sum(route_hits, axis=1).astype(jnp.bfloat16)
    dispatched = jnp.einsum(
        "ts,td->sd", picker, normalized, preferred_element_type=jnp.float32
    ).astype(jnp.bfloat16)
    outgoing = dispatched.reshape(experts, capacity, D)
    arrived = lax.all_to_all(outgoing, ("exp", "head"), split_axis=0, concat_axis=0, tiled=True)
    rows_in = arrived.reshape(experts * capacity, D)
    gate_local = w_gate[0]
    up_local = w_up[0]
    down_local = w_down[0]
    shard_rows = lax.all_gather(rows_in, "ctx", axis=0, tiled=True)
    gate_part = jnp.dot(shard_rows, gate_local, preferred_element_type=jnp.float32)
    up_part = jnp.dot(shard_rows, up_local, preferred_element_type=jnp.float32)
    hidden_cols = (jax.nn.silu(gate_part) * up_part).astype(jnp.bfloat16)
    expert_cols = jnp.dot(
        lax.all_gather(hidden_cols, "ctx", axis=1, tiled=True),
        down_local,
        preferred_element_type=jnp.float32,
    ).astype(jnp.bfloat16)
    returned = lax.all_to_all(
        expert_cols.reshape(ctx_count, experts * capacity, down_local.shape[1]),
        "ctx",
        split_axis=0,
        concat_axis=2,
        tiled=True,
    )
    returned_rows = lax.all_to_all(
        returned.reshape(experts, capacity, D),
        ("exp", "head"),
        split_axis=0,
        concat_axis=0,
        tiled=True,
    )
    returned_rows = returned_rows.reshape(experts * capacity, D)
    weighted = jnp.sum(route_hits * route_weights[:, :, None], axis=1)
    moe_sum = jnp.dot(weighted, returned_rows.astype(jnp.float32), precision=lax.Precision.HIGHEST)
    return (residual_sum + moe_sum).astype(jnp.bfloat16)


def solution(mesh):
    placed = (
        P(("groups", "ctx"), None),
        P(("groups", "ctx"), ("exp", "head")),
        P(None, ("exp", "head")),
        P(None, ("exp", "head")),
        P(("exp", "head"), "ctx"),
        P(("groups", "ctx", "exp", "head"), None),
        P(),
        P(("exp", "head"), None, "ctx"),
        P(("exp", "head"), None, "ctx"),
        P(("exp", "head"), None, "ctx"),
        P(("groups", "ctx", "exp", "head"), None),
        P(("groups", "ctx", "exp", "head"), None),
    )
    return jax.shard_map(
        shards,
        mesh=mesh,
        in_specs=placed,
        out_specs=P(("groups", "ctx", "exp", "head"), None),
        check_vma=False,
    )
```

profile of v0, /device:TPU:0, one launch (start us, length us, event | category | flops | bytes accessed | tf_op | source)
XLA Modules:
  0.0 148.9 jit_solution(2626256943590443223)
XLA Ops:
  6.6 1.0 reshape.85
  7.7 15.3 %all_gather.12 = bf16[128,576]{1,0:T(8,128)(2,1)S(1)} all-gather(bf16[32,576]{1,0:T(8,128)(2,1)} %param.12), channel_id=1, replica_groups=mesh['groups'=2,'ctx'=4,'exp'=2,'head'=2] {'ctx'}, dimensions={0}, use_global_device_ids=true | all-gather | bytes 184320 | tf_op jit(solution)/shard_map/all_gather | solution.py:37
  23.1 1.3 fusion.19
  24.4 1.3 fusion.18
  25.8 0.3 select_reduce_fusion
  26.3 0.3 fusion.23
  26.7 13.5 %all_gather.13 = bf16[128,512]{1,0:T(8,128)(2,1)S(1)} all-gather(bf16[32,512]{1,0:T(8,128)(2,1)S(1)} %bitcast.80), channel_id=1, replica_groups=mesh['groups'=2,'ctx'=4,'exp'=2,'head'=2] {'ctx'}, dimensions={0}, use_global_device_ids=true | all-gather | bytes 163840 | tf_op jit(solution)/shard_map/all_gather | solution.py:73
  40.2 0.3 convolution_convert_fusion.1
  40.6 0.7 copy.57
  42.0 20.7 %reduce-scatter.4.cloned.1.call-done = bf16[8,3584]{1,0:T(8,128)(2,1)} async-done(((bf16[32,3584]{1,0:T(8,128)(2,1)}), bf16[8,3584]{1,0:T(8,128)(2,1)}) %reduce-scatter.4.cloned.1.call-update) | async-done | bytes 57360
  62.7 0.8 reshape.97
  63.5 0.6 copy.50
  64.2 4.6 %all-to-all-start = ((bf16[4,8,896]{2,1,0:T(8,128)(2,1)}), bf16[4,8,896]{2,1,0:T(8,128)(2,1)S(1)}, u32[]{:S(2)}, u32[]{:S(2)}) async-start(bf16[4,8,896]{2,1,0:T(8,128)(2,1)} %copy.50), calls=%async_computation | async-start | bytes 114688 | tf_op jit(solution)/shard_map/all_to_all | solution.py:79
  68.9 5.6 %all-to-all-done = bf16[4,8,896]{2,1,0:T(8,128)(2,1)S(1)} async-done(((bf16[4,8,896]{2,1,0:T(8,128)(2,1)}), bf16[4,8,896]{2,1,0:T(8,128)(2,1)S(1)}, u32[]{:S(2)}, u32[]{:S(2)}) %all-to-all-start) | async-done | bytes 57376 | tf_op jit(solution)/shard_map/all_to_all | solution.py:79
  74.7 0.3 fusion.1
  75.0 8.2 %all_to_all.34 = bf16[4,8,3584]{2,1,0:T(8,128)(2,1)S(1)} all-to-all(bf16[4,8,3584]{2,1,0:T(8,128)(2,1)S(1)} %fusion.1), channel_id=1, replica_groups=mesh['groups'=2,'ctx'=4,'exp'=2,'head'=2] {'exp','head'}, dimensions={0} | all-to-all | bytes 458752 | tf_op jit(solution)/shard_map/all_to_all | solution.py:100
  83.2 19.0 %all_gather.14 = bf16[128,3584]{1,0:T(8,128)(2,1)S(1)} all-gather(bf16[32,3584]{1,0:T(8,128)(2,1)S(1)} %bitcast.77), channel_id=1, replica_groups=mesh['groups'=2,'ctx'=4,'exp'=2,'head'=2] {'ctx'}, dimensions={0}, use_global_device_ids=true | all-gather | bytes 1146880 | tf_op jit(solution)/shard_map/all_gather | solution.py:105
  102.2 2.7 %fusion.7 = f32[128,512]{1,0:T(8,128)S(1)} fusion(bf16[128,3584]{1,0:T(8,128)(2,1)S(1)} %all_gather.14, bf16[1,3584,512]{2,1,0:T(8,128)(2,1)} %param.19), kind=kOutput, calls=%fused_computation.9 | convolution fusion | flops 469762048 | bytes 4849664 | tf_op jit(solution)/shard_map/dot_general | solution.py:106
  104.9 0.6 fusion.15
  105.6 15.7 %all_gather.15 = bf16[128,2048]{1,0:T(8,128)(2,1)S(1)} all-gather(bf16[128,512]{1,0:T(8,128)(2,1)S(1)} %fusion.15), channel_id=1, replica_groups=mesh['groups'=2,'ctx'=4,'exp'=2,'head'=2] {'ctx'}, dimensions={1}, use_global_device_ids=true | all-gather | bytes 655360 | tf_op jit(solution)/shard_map/all_gather | solution.py:110
  121.3 0.7 fusion.9
  122.0 10.9 %all_to_all.35 = bf16[4,32,896]{2,1,0:T(8,128)(2,1)S(1)} all-to-all(bf16[4,32,896]{2,1,0:T(8,128)(2,1)S(1)} %bitcast.78), channel_id=1, replica_groups=mesh['groups'=2,'ctx'=4,'exp'=2,'head'=2] {'ctx'}, dimensions={0} | all-to-all | bytes 458752 | tf_op jit(solution)/shard_map/all_to_all | solution.py:114
  133.1 8.1 %all_to_all.36 = bf16[4,8,3584]{2,1,0:T(8,128)(2,1)S(1)} all-to-all(bf16[4,8,3584]{2,1,0:T(8,128)(2,1)S(1)} %reshape.91), channel_id=1, replica_groups=mesh['groups'=2,'ctx'=4,'exp'=2,'head'=2] {'exp','head'}, dimensions={0} | all-to-all | bytes 458752 | tf_op jit(solution)/shard_map/all_to_all | solution.py:121
  141.2 0.8 fusion.2
  (39 shorter events, 1.8 us)
Async XLA Ops:
  6.5 33.6 %copy-start = (bf16[512,896]{1,0:T(8,128)(2,1)S(1)}, bf16[512,896]{1,0:T(8,128)(2,1)}, u32[]{:S(2)}) copy-start(bf16[512,896]{1,0:T(8,128)(2,1)} %param.16) | copy-start | bytes 2752516
  6.5 34.8 %copy-start.4 = (s32[8,2]{0,1:T(2,128)S(1)}, s32[8,2]{0,1:T(2,128)}, u32[]{:S(2)}) copy-start(s32[8,2]{0,1:T(2,128)} %param.22) | copy-start | bytes 196
  6.5 62.3 %copy-start.5 = (f32[8,2]{0,1:T(2,128)S(1)}, f32[8,2]{0,1:T(2,128)}, u32[]{:S(2)}) copy-start(f32[8,2]{0,1:T(2,128)} %param.23) | copy-start | bytes 196
  6.5 68.0 %copy-start.2 = (bf16[8,3584]{1,0:T(8,128)(2,1)S(1)}, bf16[8,3584]{1,0:T(8,128)(2,1)}, u32[]{:S(2)}) copy-start(bf16[8,3584]{1,0:T(8,128)(2,1)} %param.17) | copy-start | bytes 172036
  6.5 68.2 %copy-start.3 = (f32[3584]{0:T(1024)S(1)}, f32[3584]{0:T(1024)}, u32[]{:S(2)}) copy-start(f32[3584]{0:T(1024)} %param.18) | copy-start | bytes 43012
  6.5 56.2 %reduce-scatter.4.cloned.1.call-start = ((), (), s32[]{:S(2)}) async-start(), calls=%async_computation.5 | async-start | bytes 286720
  64.2 10.3 %all-to-all-start = ((bf16[4,8,896]{2,1,0:T(8,128)(2,1)}), bf16[4,8,896]{2,1,0:T(8,128)(2,1)S(1)}, u32[]{:S(2)}, u32[]{:S(2)}) async-start(bf16[4,8,896]{2,1,0:T(8,128)(2,1)} %copy.50), calls=%async_computation | async-start | bytes 114688 | tf_op jit(solution)/shard_map/all_to_all | solution.py:79
  74.5 30.4 %copy-start.6 = (bf16[1,3584,512]{2,1,0:T(8,128)(2,1)S(1)}, bf16[1,3584,512]{2,1,0:T(8,128)(2,1)}, u32[]{:S(2)}) copy-start(bf16[1,3584,512]{2,1,0:T(8,128)(2,1)} %param.20) | copy-start | bytes 11010052
  104.9 16.4 %copy-start.1 = (bf16[1,2048,896]{2,1,0:T(8,128)(2,1)S(1)}, bf16[1,2048,896]{2,1,0:T(8,128)(2,1)}, u32[]{:S(2)}) copy-start(bf16[1,2048,896]{2,1,0:T(8,128)(2,1)} %param.21) | copy-start | bytes 11010052
Sparse Core Ops, SparseCore 0:
  41.5 21.1 reduce-scatter.3
where the time goes:
time: 149 us
  blocking collectives  90.7 us (61%)
  waiting for transfers between devices  26.4 us (18%)
  between operations  13.6 us (9%)
  matrix products  8.66 us (6%)
  starting transfers between devices  4.66 us (3%)
  local copies, waits for them, and re-layouts  3.88 us (3%)
    unnamed x2, waiting for transfers between devices  20.7 us
    all_gather x1, blocking collectives, shards(): shard_rows = lax.all_gather(rows_in, 'ctx', axis=0, tiled=True)  19 us
    all_gather x1, blocking collectives, shards(): lax.all_gather(hidden_cols, 'ctx', axis=1, tiled=True)  15.7 us
    all_gather x1, blocking collectives, shards(): shard_rows = lax.all_gather(latent, 'ctx', axis=0, tiled=True)  15.3 us
    all_gather x1, blocking collectives, shards(): lax.all_gather(attended, 'ctx', axis=0, tiled=True)  13.5 us
    all_to_all x1, blocking collectives, shards(): lax.all_to_all(expert_cols.reshape(ctx_count, experts * capacity, down_lo...  10.9 us
    all_to_all x1, blocking collectives, shards(): lax.all_to_all(outgoing, ('exp', 'head'), split_axis=0, concat_axis=0, ti...  8.19 us
    all_to_all x1, blocking collectives, shards(): lax.all_to_all(returned.reshape(experts, capacity, D), ('exp', 'head'), s...  8.06 us
  transfers between devices with their start and end apart: 2, of which 2 were waited for; matrix products, arithmetic and copies ran while one was open for 0% of the time, Pallas kernels for 0%

commit v1 on v0

v1 whole, which is shorter than its diff:
```python
import math

import jax
import jax.numpy as jnp
from jax import lax
from jax.sharding import PartitionSpec as P

NOPE = 128
ROPE = 64
LATENT = 512
EH = ("exp", "head")
F32 = jnp.float32
BF16 = jnp.bfloat16


def send(value, axis, step):
    size = lax.axis_size(axis)
    return lax.ppermute(value, axis, [(i, (i + step) % size) for i in range(size)])


def ordered(pieces, me):
    size = len(pieces)
    stacked = jnp.stack(pieces)
    return [
        lax.dynamic_index_in_dim(stacked, (me - b) % size, 0, keepdims=False) for b in range(size)
    ]


def attend(query, latent, w_uk, w_uv, block_ids, qblock):
    rows = query.shape[0]
    head_width = NOPE + ROPE
    heads = query.shape[1] // head_width
    scale = 1.0 / math.sqrt(head_width)
    pos = (block_ids[:, None] * qblock + jnp.arange(qblock, dtype=jnp.int32)[None, :]).reshape(-1)
    compressed, rope_keys = latent[:, :LATENT], latent[:, LATENT:]
    keys = jnp.dot(compressed, w_uk, preferred_element_type=F32).astype(BF16)
    values = jnp.dot(compressed, w_uv, preferred_element_type=F32).astype(BF16)

    def part(query_rows, query_pos):
        allowed = pos[None, :] <= query_pos[:, None]
        out = []
        for h in range(heads):
            q = query_rows[:, h * head_width : (h + 1) * head_width]
            k = keys[:, h * NOPE : (h + 1) * NOPE]
            scores = jnp.einsum("qd,kd->qk", q[:, :NOPE], k, preferred_element_type=F32)
            scores = scores + jnp.einsum(
                "qd,kd->qk", q[:, NOPE:], rope_keys, preferred_element_type=F32
            )
            scores = jnp.where(allowed, scores * scale, -1e30)
            top = jnp.max(scores, axis=1, keepdims=True)
            exponent = jnp.where(allowed, jnp.exp(scores - top), 0.0)
            total = jnp.sum(exponent, axis=1, keepdims=True)
            summed = jnp.dot(
                exponent.astype(BF16),
                values[:, h * NOPE : (h + 1) * NOPE],
                preferred_element_type=F32,
            )
            out.append((summed / total).astype(BF16))
        return jnp.concatenate(out, axis=1)

    tile = rows if rows <= 256 else 128
    if tile == rows:
        return part(query, pos)
    done = lax.map(
        lambda a: part(*a), (query.reshape(-1, tile, query.shape[1]), pos.reshape(-1, tile))
    )
    return done.reshape(rows, heads * NOPE)


def shards(
    latent,
    query,
    w_uk,
    w_uv,
    w_o,
    resid,
    norm_gain,
    w_gate,
    w_up,
    w_down,
    expert_ids,
    route_weights,
):
    ctx = lax.axis_size("ctx")
    groups = lax.axis_size(EH)
    me = lax.axis_index("ctx")
    mine = lax.axis_index(EH)
    qblock = query.shape[0]
    tok = resid.shape[0]
    cols = w_o.shape[1]
    width = resid.shape[1]
    ff = w_gate.shape[2]

    packed = jnp.concatenate([query, latent], axis=1)
    pieces = [packed] + [send(packed, "ctx", d) for d in range(1, ctx)]

    experts = jnp.arange(groups, dtype=jnp.int32)
    dense = jnp.sum(
        jnp.where(expert_ids[:, :, None] == experts, route_weights[:, :, None], 0.0), axis=1
    )
    resid_cols = resid.reshape(tok, ctx, cols).transpose(1, 0, 2)
    resid_parts, dense_parts = [], []
    for d in range(ctx):
        part = lax.dynamic_index_in_dim(resid_cols, (me + d) % ctx, 0, keepdims=False)
        resid_parts.append(send(part, "ctx", d) if d else part)
        dense_parts.append(send(dense, "ctx", d) if d else dense)

    gathered = jnp.concatenate(pieces, axis=0)
    block_ids = (me - jnp.arange(ctx, dtype=jnp.int32)) % ctx
    attended = attend(
        gathered[:, : query.shape[1]],
        gathered[:, query.shape[1] :],
        w_uk,
        w_uv,
        block_ids,
        qblock,
    )
    partial = jnp.dot(attended, w_o, preferred_element_type=F32).astype(BF16)
    partial = partial.reshape(ctx, groups, tok, cols)
    total = 0.0
    for s in range(groups):
        part = lax.dynamic_index_in_dim(partial, (mine + s) % groups, 1, keepdims=False)
        total = total + (send(part, EH, s) if s else part).astype(F32)
    total = total + jnp.stack(resid_parts).astype(F32)
    residual_sum = jnp.stack(ordered([total[d] for d in range(ctx)], me))
    dense_rows = jnp.concatenate(ordered(dense_parts, me), axis=0)

    travelling = residual_sum.astype(BF16).reshape(ctx * tok, cols)
    columns = [travelling] + [send(travelling, "ctx", d) for d in range(1, ctx)]
    rows = jnp.concatenate(ordered(columns, me), axis=1).astype(F32)
    inverse_rms = lax.rsqrt(jnp.mean(rows * rows, axis=1, keepdims=True) + 1e-06)
    normalized = (rows * inverse_rms * norm_gain).astype(BF16)
    everything = lax.all_gather(normalized, EH, axis=0, tiled=True)

    gate_part = jnp.dot(everything, w_gate[0], preferred_element_type=F32)
    up_part = jnp.dot(everything, w_up[0], preferred_element_type=F32)
    hidden = (jax.nn.silu(gate_part) * up_part).astype(BF16)
    hidden = [hidden] + [send(hidden, "ctx", d) for d in range(1, ctx)]
    hidden = jnp.concatenate(ordered(hidden, me), axis=1)
    expert_cols = jnp.dot(hidden, w_down[0], preferred_element_type=F32).astype(BF16)
    expert_cols = expert_cols.reshape(groups, ctx * tok, cols)
    moe = 0.0
    for s in range(groups):
        part = lax.dynamic_index_in_dim(expert_cols, (mine + s) % groups, 0, keepdims=False)
        part = (send(part, EH, s) if s else part).astype(F32)
        weight = lax.dynamic_slice_in_dim(dense_rows, (mine - s) % groups, 1, axis=1)
        moe = moe + part * weight
    final = (residual_sum.reshape(ctx * tok, cols) + moe).astype(BF16).reshape(ctx, tok, cols)
    out = []
    for d in range(ctx):
        part = lax.dynamic_index_in_dim(final, (me + d) % ctx, 0, keepdims=False)
        out.append(send(part, "ctx", d) if d else part)
    return jnp.concatenate(ordered(out, me), axis=1)


def solution(mesh):
    placed = (
        P(("groups", "ctx"), None),
        P(("groups", "ctx"), ("exp", "head")),
        P(None, ("exp", "head")),
        P(None, ("exp", "head")),
        P(("exp", "head"), "ctx"),
        P(("groups", "ctx", "exp", "head"), None),
        P(),
        P(("exp", "head"), None, "ctx"),
        P(("exp", "head"), None, "ctx"),
        P(("exp", "head"), None, "ctx"),
        P(("groups", "ctx", "exp", "head"), None),
        P(("groups", "ctx", "exp", "head"), None),
    )
    return jax.shard_map(
        shards,
        mesh=mesh,
        in_specs=placed,
        out_specs=P(("groups", "ctx", "exp", "head"), None),
        check_vma=False,
    )
```

time: 149 us -> 74.2 us (0.50)
  blocking collectives: 90.7 us -> 9.2 us
  starting transfers between devices: 4.66 us -> 35.1 us
  between operations: 13.6 us -> 0.46 us
  waiting for transfers between devices: 26.4 us -> 17.4 us
    all_gather x4 -> x1, blocking collectives: 63.6 us -> 9.2 us  [shards(): everything = lax.all_gather(normalized, EH, axis=0, tiled=True)]
    ppermute x0 -> x24, starting transfers between devices: none -> 35.1 us  [send(): lax.ppermute(value, axis, [(i, (i + step) % size) for i in range(size)])]
    all_to_all x3 -> x0, blocking collectives: 27.1 us -> none  [the longest x1 10.9 us: shards(): lax.all_to_all(expert_cols.reshape(ctx_count, experts * capacity, down_lo...]
    unnamed x2 -> x0, waiting for transfers between devices: 20.7 us -> none
    ppermute x0 -> x24, waiting for transfers between devices: none -> 17.4 us  [send(): lax.ppermute(value, axis, [(i, (i + step) % size) for i in range(size)])]
    all_to_all x1 -> x0, waiting for transfers between devices: 5.64 us -> none  [shards(): lax.all_to_all(summed.astype(jnp.bfloat16), 'ctx', split_axis=0, concat_a...]
    all_to_all x1 -> x0, starting transfers between devices: 4.62 us -> none  [shards(): lax.all_to_all(summed.astype(jnp.bfloat16), 'ctx', split_axis=0, concat_a...]
    dot_general x11 -> x18, matrix products: 8.66 us -> 7.51 us  [the longest x1 1.27 us: attend(): keys = jnp.dot(compressed, w_uk, preferred_element_type=F32).astype(BF16)]
  transfers between devices with their start and end apart: 2 -> 24, of which waited for: 2 -> 8; matrix products, arithmetic and copies ran while one was open for 0% -> 9% of each run, Pallas kernels for 0% -> 0%
where the time goes in v1:
time: 74.2 us; the launch traced here: 73.9 us
  starting transfers between devices  35.1 us (47%)
  waiting for transfers between devices  17.4 us (23%)
  blocking collectives  9.2 us (12%)
  matrix products  7.51 us (10%)
  local copies, waits for them, and re-layouts  2.77 us (4%)
  other arithmetic  1.54 us (2%)
    ppermute x24, starting transfers between devices, send(): lax.ppermute(value, axis, [(i, (i + step) % size) for i in range(size)])  35.1 us
    ppermute x24, waiting for transfers between devices, send(): lax.ppermute(value, axis, [(i, (i + step) % size) for i in range(size)])  17.4 us
    all_gather x1, blocking collectives, shards(): everything = lax.all_gather(normalized, EH, axis=0, tiled=True)  9.2 us
  transfers between devices with their start and end apart: 24, of which 8 were waited for; matrix products, arithmetic and copies ran while one was open for 9% of the time, Pallas kernels for 0%

profile of v1, /device:TPU:0, one launch (start us, length us, event | category | flops | bytes accessed | tf_op | source)
XLA Modules:
  0.0 73.9 jit_solution(11021789016909802376)
XLA Ops:
  1.7 3.0 %collective-permute-start = (bf16[32,1344]{1,0:T(8,128)(2,1)S(1)}, bf16[32,1344]{1,0:T(8,128)(2,1)S(1)}, u32[]{:S(2)}, u32[]{:S(2)}) collective-permute-start(bf16[32,1344]{1,0:T(8,128)(2,1)S(1)} %constant_dynamic-update-slice_fusion), channel_id=1, source_target_pairs={{0,4},{4,8},{8,12},{12,0},{1,5},{5,9},{9,13},{13,1},{2,6},{6,10},{... | collective-permute-start | bytes 258056 | tf_op jit(solution)/shard_map/ppermute | solution.py:18
  4.7 2.6 %collective-permute-start.1 = (bf16[32,1344]{1,0:T(8,128)(2,1)S(1)}, bf16[32,1344]{1,0:T(8,128)(2,1)S(1)}, u32[]{:S(2)}, u32[]{:S(2)}) collective-permute-start(bf16[32,1344]{1,0:T(8,128)(2,1)S(1)} %constant_dynamic-update-slice_fusion), channel_id=1, source_target_pairs={{0,8},{4,12},{8,0},{12,4},{1,9},{5,13},{9,1},{13,5},{2,10},{6,14},... | collective-permute-start | bytes 258056 | tf_op jit(solution)/shard_map/ppermute | solution.py:18
  7.3 1.3 %collective-permute-start.2 = (bf16[32,1344]{1,0:T(8,128)(2,1)S(1)}, bf16[32,1344]{1,0:T(8,128)(2,1)S(1)}, u32[]{:S(2)}, u32[]{:S(2)}) collective-permute-start(bf16[32,1344]{1,0:T(8,128)(2,1)S(1)} %constant_dynamic-update-slice_fusion), channel_id=1, source_target_pairs={{0,12},{4,0},{8,4},{12,8},{1,13},{5,1},{9,5},{13,9},{2,14},{6,2},{... | collective-permute-start | bytes 258056 | tf_op jit(solution)/shard_map/ppermute | solution.py:18
  9.6 2.9 %collective-permute-start.8 = (bf16[8,896]{1,0:T(8,128)(2,1)S(1)}, bf16[8,896]{1,0:T(8,128)(2,1)S(1)}, u32[]{:S(2)}, u32[]{:S(2)}) collective-permute-start(bf16[8,896]{1,0:T(8,128)(2,1)S(1)} %get-tuple-element.38), channel_id=1, source_target_pairs={{0,12},{4,0},{8,4},{12,8},{1,13},{5,1},{9,5},{13,9},{2,14},{6,2},{... | collective-permute-start | bytes 43016 | tf_op jit(solution)/shard_map/ppermute | solution.py:18
  13.7 1.3 %convolution_convert_fusion.2 = bf16[128,512]{1,0:T(8,128)(2,1)S(1)} fusion(bf16[512,512]{1,0:T(8,128)(2,1)} %param.14, bf16[128,1344]{1,0:T(8,128)(2,1)S(1)} %pad_maximum_fusion.1), kind=kOutput, calls=%fused_computation.11 | convolution fusion | flops 67174400 | bytes 786432 | tf_op jit(solution)/shard_map/dot_general | solution.py:36
  15.0 1.3 %convolution_convert_fusion.1 = bf16[128,512]{1,0:T(8,128)(2,1)S(1)} fusion(bf16[512,512]{1,0:T(8,128)(2,1)} %param.15, bf16[128,1344]{1,0:T(8,128)(2,1)S(1)} %pad_maximum_fusion.1), kind=kOutput, calls=%fused_computation.10 | convolution fusion | flops 67174400 | bytes 786432 | tf_op jit(solution)/shard_map/dot_general | solution.py:37
  19.5 1.6 %collective-permute-start.4 = (bf16[4,8,896]{2,1,0:T(8,128)(2,1)S(1)}, bf16[4,8,896]{2,1,0:T(8,128)(2,1)S(1)}, u32[]{:S(2)}, u32[]{:S(2)}) collective-permute-start(bf16[4,8,896]{2,1,0:T(8,128)(2,1)S(1)} %get-tuple-element.22), channel_id=1, source_target_pairs={{0,2},{1,3},{2,0},{3,1},{4,6},{5,7},{6,4},{7,5},{8,10},{9,11},{10,... | collective-permute-start | bytes 172040 | tf_op jit(solution)/shard_map/ppermute | solution.py:18
  21.1 1.4 %collective-permute-start.5 = (bf16[4,8,896]{2,1,0:T(8,128)(2,1)S(1)}, bf16[4,8,896]{2,1,0:T(8,128)(2,1)S(1)}, u32[]{:S(2)}, u32[]{:S(2)}) collective-permute-start(bf16[4,8,896]{2,1,0:T(8,128)(2,1)S(1)} %get-tuple-element.21), channel_id=1, source_target_pairs={{0,3},{1,0},{2,1},{3,2},{4,7},{5,4},{6,5},{7,6},{8,11},{9,8},{10,9... | collective-permute-start | bytes 172040 | tf_op jit(solution)/shard_map/ppermute | solution.py:18
  22.6 2.5 %collective-permute-start.15 = (f32[8,4]{0,1:T(4,128)S(1)}, f32[8,4]{0,1:T(4,128)S(1)}, u32[]{:S(2)}, u32[]{:S(2)}) collective-permute-start(f32[8,4]{0,1:T(4,128)S(1)} %select_reduce_fusion), channel_id=1, source_target_pairs={{0,4},{4,8},{8,12},{12,0},{1,5},{5,9},{9,13},{13,1},{2,6},{6,10},{... | collective-permute-start | bytes 392 | tf_op jit(solution)/shard_map/ppermute | solution.py:18
  25.2 2.1 %collective-permute-start.16 = (f32[8,4]{0,1:T(4,128)S(1)}, f32[8,4]{0,1:T(4,128)S(1)}, u32[]{:S(2)}, u32[]{:S(2)}) collective-permute-start(f32[8,4]{0,1:T(4,128)S(1)} %select_reduce_fusion), channel_id=1, source_target_pairs={{0,8},{4,12},{8,0},{12,4},{1,9},{5,13},{9,1},{13,5},{2,10},{6,14},... | collective-permute-start | bytes 392 | tf_op jit(solution)/shard_map/ppermute | solution.py:18
  27.7 1.7 %collective-permute-start.9 = (bf16[32,896]{1,0:T(8,128)(2,1)S(1)}, bf16[32,896]{1,0:T(8,128)(2,1)S(1)}, u32[]{:S(2)}, u32[]{:S(2)}) collective-permute-start(bf16[32,896]{1,0:T(8,128)(2,1)S(1)} %get-tuple-element.24), channel_id=1, source_target_pairs={{0,4},{4,8},{8,12},{12,0},{1,5},{5,9},{9,13},{13,1},{2,6},{6,10},{... | collective-permute-start | bytes 172040 | tf_op jit(solution)/shard_map/ppermute | solution.py:18
  30.3 1.6 %collective-permute-start.11 = (bf16[32,896]{1,0:T(8,128)(2,1)S(1)}, bf16[32,896]{1,0:T(8,128)(2,1)S(1)}, u32[]{:S(2)}, u32[]{:S(2)}) collective-permute-start(bf16[32,896]{1,0:T(8,128)(2,1)S(1)} %get-tuple-element.24), channel_id=1, source_target_pairs={{0,12},{4,0},{8,4},{12,8},{1,13},{5,1},{9,5},{13,9},{2,14},{6,2},{... | collective-permute-start | bytes 172040 | tf_op jit(solution)/shard_map/ppermute | solution.py:18
  31.9 1.9 %collective-permute-done.9 = bf16[32,896]{1,0:T(8,128)(2,1)S(1)} collective-permute-done((bf16[32,896]{1,0:T(8,128)(2,1)S(1)}, bf16[32,896]{1,0:T(8,128)(2,1)S(1)}, u32[]{:S(2)}, u32[]{:S(2)}) %collective-permute-start.9) | collective-permute-done | bytes 57376 | tf_op jit(solution)/shard_map/ppermute | solution.py:18
  33.8 1.3 %collective-permute-done.10 = bf16[32,896]{1,0:T(8,128)(2,1)S(1)} collective-permute-done((bf16[32,896]{1,0:T(8,128)(2,1)S(1)}, bf16[32,896]{1,0:T(8,128)(2,1)S(1)}, u32[]{:S(2)}, u32[]{:S(2)}) %collective-permute-start.10) | collective-permute-done | bytes 57376 | tf_op jit(solution)/shard_map/ppermute | solution.py:18
  35.5 9.2 %all_gather.3 = bf16[128,3584]{1,0:T(8,128)(2,1)S(1)} all-gather(bf16[32,3584]{1,0:T(8,128)(2,1)S(1)} %fusion.36), channel_id=1, replica_groups=mesh['groups'=2,'ctx'=4,'exp'=2,'head'=2] {'exp','head'}, dimensions={0}, use_global_device_ids=true | all-gather | bytes 1146880 | tf_op jit(solution)/shard_map/all_gather | solution.py:133
  46.0 1.2 %collective-permute-start.12 = (bf16[128,512]{1,0:T(8,128)(2,1)S(1)}, bf16[128,512]{1,0:T(8,128)(2,1)S(1)}, u32[]{:S(2)}, u32[]{:S(2)}) collective-permute-start(bf16[128,512]{1,0:T(8,128)(2,1)S(1)} %fusion.12), channel_id=1, source_target_pairs={{0,4},{4,8},{8,12},{12,0},{1,5},{5,9},{9,13},{13,1},{2,6},{6,10},{... | collective-permute-start | bytes 393224 | tf_op jit(solution)/shard_map/ppermute | solution.py:18
  47.3 2.0 %collective-permute-start.13 = (bf16[128,512]{1,0:T(8,128)(2,1)S(1)}, bf16[128,512]{1,0:T(8,128)(2,1)S(1)}, u32[]{:S(2)}, u32[]{:S(2)}) collective-permute-start(bf16[128,512]{1,0:T(8,128)(2,1)S(1)} %fusion.12), channel_id=1, source_target_pairs={{0,8},{4,12},{8,0},{12,4},{1,9},{5,13},{9,1},{13,5},{2,10},{6,14},... | collective-permute-start | bytes 393224 | tf_op jit(solution)/shard_map/ppermute | solution.py:18
  50.0 4.3 %collective-permute-done.12 = bf16[128,512]{1,0:T(8,128)(2,1)S(1)} collective-permute-done((bf16[128,512]{1,0:T(8,128)(2,1)S(1)}, bf16[128,512]{1,0:T(8,128)(2,1)S(1)}, u32[]{:S(2)}, u32[]{:S(2)}) %collective-permute-start.12) | collective-permute-done | bytes 131104 | tf_op jit(solution)/shard_map/ppermute | solution.py:18
  54.3 5.0 %collective-permute-done.13 = bf16[128,512]{1,0:T(8,128)(2,1)S(1)} collective-permute-done((bf16[128,512]{1,0:T(8,128)(2,1)S(1)}, bf16[128,512]{1,0:T(8,128)(2,1)S(1)}, u32[]{:S(2)}, u32[]{:S(2)}) %collective-permute-start.13) | collective-permute-done | bytes 131104 | tf_op jit(solution)/shard_map/ppermute | solution.py:18
  61.1 1.4 %collective-permute-start.20 = (bf16[32,896]{1,0:T(8,128)(2,1)S(1)}, bf16[32,896]{1,0:T(8,128)(2,1)S(1)}, u32[]{:S(2)}, u32[]{:S(2)}) collective-permute-start(bf16[32,896]{1,0:T(8,128)(2,1)S(1)} %get-tuple-element.14), channel_id=1, source_target_pairs={{0,3},{1,0},{2,1},{3,2},{4,7},{5,4},{6,5},{7,6},{8,11},{9,8},{10,9... | collective-permute-start | bytes 172040 | tf_op jit(solution)/shard_map/ppermute | solution.py:18
  62.5 1.3 %collective-permute-done.18 = bf16[32,896]{1,0:T(8,128)(2,1)S(1)} collective-permute-done((bf16[32,896]{1,0:T(8,128)(2,1)S(1)}, bf16[32,896]{1,0:T(8,128)(2,1)S(1)}, u32[]{:S(2)}, u32[]{:S(2)}) %collective-permute-start.18) | collective-permute-done | bytes 57376 | tf_op jit(solution)/shard_map/ppermute | solution.py:18
  65.3 3.3 %collective-permute-start.21 = (bf16[8,896]{1,0:T(8,128)(2,1)S(1)}, bf16[8,896]{1,0:T(8,128)(2,1)S(1)}, u32[]{:S(2)}, u32[]{:S(2)}) collective-permute-start(bf16[8,896]{1,0:T(8,128)(2,1)S(1)} %get-tuple-element.36), channel_id=1, source_target_pairs={{0,4},{4,8},{8,12},{12,0},{1,5},{5,9},{9,13},{13,1},{2,6},{6,10},{... | collective-permute-start | bytes 43016 | tf_op jit(solution)/shard_map/ppermute | solution.py:18
  68.6 2.5 %collective-permute-start.23 = (bf16[8,896]{1,0:T(8,128)(2,1)S(1)}, bf16[8,896]{1,0:T(8,128)(2,1)S(1)}, u32[]{:S(2)}, u32[]{:S(2)}) collective-permute-start(bf16[8,896]{1,0:T(8,128)(2,1)S(1)} %get-tuple-element.34), channel_id=1, source_target_pairs={{0,12},{4,0},{8,4},{12,8},{1,13},{5,1},{9,5},{13,9},{2,14},{6,2},{... | collective-permute-start | bytes 43016 | tf_op jit(solution)/shard_map/ppermute | solution.py:18
  71.1 2.2 %collective-permute-done.22 = bf16[8,896]{1,0:T(8,128)(2,1)S(1)} collective-permute-done((bf16[8,896]{1,0:T(8,128)(2,1)S(1)}, bf16[8,896]{1,0:T(8,128)(2,1)S(1)}, u32[]{:S(2)}, u32[]{:S(2)}) %collective-permute-start.22) | collective-permute-done | bytes 14368 | tf_op jit(solution)/shard_map/ppermute | solution.py:18
  (87 shorter events, 14.6 us)
Async XLA Ops:
  1.7 11.0 %collective-permute-start = (bf16[32,1344]{1,0:T(8,128)(2,1)S(1)}, bf16[32,1344]{1,0:T(8,128)(2,1)S(1)}, u32[]{:S(2)}, u32[]{:S(2)}) collective-permute-start(bf16[32,1344]{1,0:T(8,128)(2,1)S(1)} %constant_dynamic-update-slice_fusion), channel_id=1, source_target_pairs={{0,4},{4,8},{8,12},{12,0},{1,5},{5,9},{9,13},{13,1},{2,6},{6,10},{... | collective-permute-start | bytes 258056 | tf_op jit(solution)/shard_map/ppermute | solution.py:18
  4.7 8.9 %collective-permute-start.1 = (bf16[32,1344]{1,0:T(8,128)(2,1)S(1)}, bf16[32,1344]{1,0:T(8,128)(2,1)S(1)}, u32[]{:S(2)}, u32[]{:S(2)}) collective-permute-start(bf16[32,1344]{1,0:T(8,128)(2,1)S(1)} %constant_dynamic-update-slice_fusion), channel_id=1, source_target_pairs={{0,8},{4,12},{8,0},{12,4},{1,9},{5,13},{9,1},{13,5},{2,10},{6,14},... | collective-permute-start | bytes 258056 | tf_op jit(solution)/shard_map/ppermute | solution.py:18
  7.3 6.4 %collective-permute-start.2 = (bf16[32,1344]{1,0:T(8,128)(2,1)S(1)}, bf16[32,1344]{1,0:T(8,128)(2,1)S(1)}, u32[]{:S(2)}, u32[]{:S(2)}) collective-permute-start(bf16[32,1344]{1,0:T(8,128)(2,1)S(1)} %constant_dynamic-update-slice_fusion), channel_id=1, source_target_pairs={{0,12},{4,0},{8,4},{12,8},{1,13},{5,1},{9,5},{13,9},{2,14},{6,2},{... | collective-permute-start | bytes 258056 | tf_op jit(solution)/shard_map/ppermute | solution.py:18
  9.4 11.7 %collective-permute-start.7 = (bf16[8,896]{1,0:T(8,128)(2,1)S(1)}, bf16[8,896]{1,0:T(8,128)(2,1)S(1)}, u32[]{:S(2)}, u32[]{:S(2)}) collective-permute-start(bf16[8,896]{1,0:T(8,128)(2,1)S(1)} %get-tuple-element.39), channel_id=1, source_target_pairs={{0,8},{4,12},{8,0},{12,4},{1,9},{5,13},{9,1},{13,5},{2,10},{6,14},... | collective-permute-start | bytes 43016 | tf_op jit(solution)/shard_map/ppermute | solution.py:18
  9.6 13.0 %collective-permute-start.8 = (bf16[8,896]{1,0:T(8,128)(2,1)S(1)}, bf16[8,896]{1,0:T(8,128)(2,1)S(1)}, u32[]{:S(2)}, u32[]{:S(2)}) collective-permute-start(bf16[8,896]{1,0:T(8,128)(2,1)S(1)} %get-tuple-element.38), channel_id=1, source_target_pairs={{0,12},{4,0},{8,4},{12,8},{1,13},{5,1},{9,5},{13,9},{2,14},{6,2},{... | collective-permute-start | bytes 43016 | tf_op jit(solution)/shard_map/ppermute | solution.py:18
  12.7 12.5 %collective-permute-start.6 = (bf16[8,896]{1,0:T(8,128)(2,1)S(1)}, bf16[8,896]{1,0:T(8,128)(2,1)S(1)}, u32[]{:S(2)}, u32[]{:S(2)}) collective-permute-start(bf16[8,896]{1,0:T(8,128)(2,1)S(1)} %get-tuple-element.40), channel_id=1, source_target_pairs={{0,4},{4,8},{8,12},{12,0},{1,5},{5,9},{9,13},{13,1},{2,6},{6,10},{... | collective-permute-start | bytes 43016 | tf_op jit(solution)/shard_map/ppermute | solution.py:18
  19.5 7.8 %collective-permute-start.3 = (bf16[4,8,896]{2,1,0:T(8,128)(2,1)S(1)}, bf16[4,8,896]{2,1,0:T(8,128)(2,1)S(1)}, u32[]{:S(2)}, u32[]{:S(2)}) collective-permute-start(bf16[4,8,896]{2,1,0:T(8,128)(2,1)S(1)} %get-tuple-element.20), channel_id=1, source_target_pairs={{0,1},{1,2},{2,3},{3,0},{4,5},{5,6},{6,7},{7,4},{8,9},{9,10},{10,1... | collective-permute-start | bytes 172040 | tf_op jit(solution)/shard_map/ppermute | solution.py:18
  19.5 8.1 %collective-permute-start.4 = (bf16[4,8,896]{2,1,0:T(8,128)(2,1)S(1)}, bf16[4,8,896]{2,1,0:T(8,128)(2,1)S(1)}, u32[]{:S(2)}, u32[]{:S(2)}) collective-permute-start(bf16[4,8,896]{2,1,0:T(8,128)(2,1)S(1)} %get-tuple-element.22), channel_id=1, source_target_pairs={{0,2},{1,3},{2,0},{3,1},{4,6},{5,7},{6,4},{7,5},{8,10},{9,11},{10,... | collective-permute-start | bytes 172040 | tf_op jit(solution)/shard_map/ppermute | solution.py:18
  21.1 6.6 %collective-permute-start.5 = (bf16[4,8,896]{2,1,0:T(8,128)(2,1)S(1)}, bf16[4,8,896]{2,1,0:T(8,128)(2,1)S(1)}, u32[]{:S(2)}, u32[]{:S(2)}) collective-permute-start(bf16[4,8,896]{2,1,0:T(8,128)(2,1)S(1)} %get-tuple-element.21), channel_id=1, source_target_pairs={{0,3},{1,0},{2,1},{3,2},{4,7},{5,4},{6,5},{7,6},{8,11},{9,8},{10,9... | collective-permute-start | bytes 172040 | tf_op jit(solution)/shard_map/ppermute | solution.py:18
  22.6 7.7 %collective-permute-start.15 = (f32[8,4]{0,1:T(4,128)S(1)}, f32[8,4]{0,1:T(4,128)S(1)}, u32[]{:S(2)}, u32[]{:S(2)}) collective-permute-start(f32[8,4]{0,1:T(4,128)S(1)} %select_reduce_fusion), channel_id=1, source_target_pairs={{0,4},{4,8},{8,12},{12,0},{1,5},{5,9},{9,13},{13,1},{2,6},{6,10},{... | collective-permute-start | bytes 392 | tf_op jit(solution)/shard_map/ppermute | solution.py:18
  25.2 6.7 %collective-permute-start.16 = (f32[8,4]{0,1:T(4,128)S(1)}, f32[8,4]{0,1:T(4,128)S(1)}, u32[]{:S(2)}, u32[]{:S(2)}) collective-permute-start(f32[8,4]{0,1:T(4,128)S(1)} %select_reduce_fusion), channel_id=1, source_target_pairs={{0,8},{4,12},{8,0},{12,4},{1,9},{5,13},{9,1},{13,5},{2,10},{6,14},... | collective-permute-start | bytes 392 | tf_op jit(solution)/shard_map/ppermute | solution.py:18
  27.3 4.6 %collective-permute-start.17 = (f32[8,4]{0,1:T(4,128)S(1)}, f32[8,4]{0,1:T(4,128)S(1)}, u32[]{:S(2)}, u32[]{:S(2)}) collective-permute-start(f32[8,4]{0,1:T(4,128)S(1)} %select_reduce_fusion), channel_id=1, source_target_pairs={{0,12},{4,0},{8,4},{12,8},{1,13},{5,1},{9,5},{13,9},{2,14},{6,2},{... | collective-permute-start | bytes 392 | tf_op jit(solution)/shard_map/ppermute | solution.py:18
  27.7 6.1 %collective-permute-start.9 = (bf16[32,896]{1,0:T(8,128)(2,1)S(1)}, bf16[32,896]{1,0:T(8,128)(2,1)S(1)}, u32[]{:S(2)}, u32[]{:S(2)}) collective-permute-start(bf16[32,896]{1,0:T(8,128)(2,1)S(1)} %get-tuple-element.24), channel_id=1, source_target_pairs={{0,4},{4,8},{8,12},{12,0},{1,5},{5,9},{9,13},{13,1},{2,6},{6,10},{... | collective-permute-start | bytes 172040 | tf_op jit(solution)/shard_map/ppermute | solution.py:18
  29.4 5.7 %collective-permute-start.10 = (bf16[32,896]{1,0:T(8,128)(2,1)S(1)}, bf16[32,896]{1,0:T(8,128)(2,1)S(1)}, u32[]{:S(2)}, u32[]{:S(2)}) collective-permute-start(bf16[32,896]{1,0:T(8,128)(2,1)S(1)} %get-tuple-element.24), channel_id=1, source_target_pairs={{0,8},{4,12},{8,0},{12,4},{1,9},{5,13},{9,1},{13,5},{2,10},{6,14},... | collective-permute-start | bytes 172040 | tf_op jit(solution)/shard_map/ppermute | solution.py:18
  30.3 4.8 %collective-permute-start.11 = (bf16[32,896]{1,0:T(8,128)(2,1)S(1)}, bf16[32,896]{1,0:T(8,128)(2,1)S(1)}, u32[]{:S(2)}, u32[]{:S(2)}) collective-permute-start(bf16[32,896]{1,0:T(8,128)(2,1)S(1)} %get-tuple-element.24), channel_id=1, source_target_pairs={{0,12},{4,0},{8,4},{12,8},{1,13},{5,1},{9,5},{13,9},{2,14},{6,2},{... | collective-permute-start | bytes 172040 | tf_op jit(solution)/shard_map/ppermute | solution.py:18
  46.0 8.3 %collective-permute-start.12 = (bf16[128,512]{1,0:T(8,128)(2,1)S(1)}, bf16[128,512]{1,0:T(8,128)(2,1)S(1)}, u32[]{:S(2)}, u32[]{:S(2)}) collective-permute-start(bf16[128,512]{1,0:T(8,128)(2,1)S(1)} %fusion.12), channel_id=1, source_target_pairs={{0,4},{4,8},{8,12},{12,0},{1,5},{5,9},{9,13},{13,1},{2,6},{6,10},{... | collective-permute-start | bytes 393224 | tf_op jit(solution)/shard_map/ppermute | solution.py:18
  47.3 12.1 %collective-permute-start.13 = (bf16[128,512]{1,0:T(8,128)(2,1)S(1)}, bf16[128,512]{1,0:T(8,128)(2,1)S(1)}, u32[]{:S(2)}, u32[]{:S(2)}) collective-permute-start(bf16[128,512]{1,0:T(8,128)(2,1)S(1)} %fusion.12), channel_id=1, source_target_pairs={{0,8},{4,12},{8,0},{12,4},{1,9},{5,13},{9,1},{13,5},{2,10},{6,14},... | collective-permute-start | bytes 393224 | tf_op jit(solution)/shard_map/ppermute | solution.py:18
  49.3 10.0 %collective-permute-start.14 = (bf16[128,512]{1,0:T(8,128)(2,1)S(1)}, bf16[128,512]{1,0:T(8,128)(2,1)S(1)}, u32[]{:S(2)}, u32[]{:S(2)}) collective-permute-start(bf16[128,512]{1,0:T(8,128)(2,1)S(1)} %fusion.12), channel_id=1, source_target_pairs={{0,12},{4,0},{8,4},{12,8},{1,13},{5,1},{9,5},{13,9},{2,14},{6,2},{... | collective-permute-start | bytes 393224 | tf_op jit(solution)/shard_map/ppermute | solution.py:18
  60.2 3.7 %collective-permute-start.18 = (bf16[32,896]{1,0:T(8,128)(2,1)S(1)}, bf16[32,896]{1,0:T(8,128)(2,1)S(1)}, u32[]{:S(2)}, u32[]{:S(2)}) collective-permute-start(bf16[32,896]{1,0:T(8,128)(2,1)S(1)} %get-tuple-element.13), channel_id=1, source_target_pairs={{0,1},{1,2},{2,3},{3,0},{4,5},{5,6},{6,7},{7,4},{8,9},{9,10},{10,1... | collective-permute-start | bytes 172040 | tf_op jit(solution)/shard_map/ppermute | solution.py:18
  60.3 4.8 %collective-permute-start.19 = (bf16[32,896]{1,0:T(8,128)(2,1)S(1)}, bf16[32,896]{1,0:T(8,128)(2,1)S(1)}, u32[]{:S(2)}, u32[]{:S(2)}) collective-permute-start(bf16[32,896]{1,0:T(8,128)(2,1)S(1)} %get-tuple-element.15), channel_id=1, source_target_pairs={{0,2},{1,3},{2,0},{3,1},{4,6},{5,7},{6,4},{7,5},{8,10},{9,11},{10,... | collective-permute-start | bytes 172040 | tf_op jit(solution)/shard_map/ppermute | solution.py:18
  61.1 4.0 %collective-permute-start.20 = (bf16[32,896]{1,0:T(8,128)(2,1)S(1)}, bf16[32,896]{1,0:T(8,128)(2,1)S(1)}, u32[]{:S(2)}, u32[]{:S(2)}) collective-permute-start(bf16[32,896]{1,0:T(8,128)(2,1)S(1)} %get-tuple-element.14), channel_id=1, source_target_pairs={{0,3},{1,0},{2,1},{3,2},{4,7},{5,4},{6,5},{7,6},{8,11},{9,8},{10,9... | collective-permute-start | bytes 172040 | tf_op jit(solution)/shard_map/ppermute | solution.py:18
  65.3 5.8 %collective-permute-start.21 = (bf16[8,896]{1,0:T(8,128)(2,1)S(1)}, bf16[8,896]{1,0:T(8,128)(2,1)S(1)}, u32[]{:S(2)}, u32[]{:S(2)}) collective-permute-start(bf16[8,896]{1,0:T(8,128)(2,1)S(1)} %get-tuple-element.36), channel_id=1, source_target_pairs={{0,4},{4,8},{8,12},{12,0},{1,5},{5,9},{9,13},{13,1},{2,6},{6,10},{... | collective-permute-start | bytes 43016 | tf_op jit(solution)/shard_map/ppermute | solution.py:18
  68.6 4.6 %collective-permute-start.22 = (bf16[8,896]{1,0:T(8,128)(2,1)S(1)}, bf16[8,896]{1,0:T(8,128)(2,1)S(1)}, u32[]{:S(2)}, u32[]{:S(2)}) collective-permute-start(bf16[8,896]{1,0:T(8,128)(2,1)S(1)} %get-tuple-element.35), channel_id=1, source_target_pairs={{0,8},{4,12},{8,0},{12,4},{1,9},{5,13},{9,1},{13,5},{2,10},{6,14},... | collective-permute-start | bytes 43016 | tf_op jit(solution)/shard_map/ppermute | solution.py:18
  68.6 4.6 %collective-permute-start.23 = (bf16[8,896]{1,0:T(8,128)(2,1)S(1)}, bf16[8,896]{1,0:T(8,128)(2,1)S(1)}, u32[]{:S(2)}, u32[]{:S(2)}) collective-permute-start(bf16[8,896]{1,0:T(8,128)(2,1)S(1)} %get-tuple-element.34), channel_id=1, source_target_pairs={{0,12},{4,0},{8,4},{12,8},{1,13},{5,1},{9,5},{13,9},{2,14},{6,2},{... | collective-permute-start | bytes 43016 | tf_op jit(solution)/shard_map/ppermute | solution.py:18
  (7 other events, 95.3 us)

commit v2 on v1

--- a/solution.py
+++ b/solution.py
@@ -1,8 +1,11 @@
+import functools
 import math
 
 import jax
 import jax.numpy as jnp
 from jax import lax
+from jax.experimental import pallas as pl
+from jax.experimental.pallas import tpu as pltpu
 from jax.sharding import PartitionSpec as P
 
 NOPE = 128
@@ -153,6 +156,276 @@
     return jnp.concatenate(ordered(out, me), axis=1)
 
 
+def lanes(ref, start, size):
+    return ref[:, pl.ds(pl.multiple_of(start * size, 128), size)]
+
+
+def call(kernel, out, args, flops, vmem):
+    return pl.pallas_call(
+        kernel,
+        out_shape=out,
+        in_specs=[pl.BlockSpec(memory_space=pltpu.VMEM)] * len(args),
+        out_specs=jax.tree.map(lambda _: pl.BlockSpec(memory_space=pltpu.VMEM), out),
+        compiler_params=pltpu.CompilerParams(vmem_limit_bytes=vmem << 20),
+        cost_estimate=pl.CostEstimate(
+            flops=flops, bytes_accessed=sum(a.size * a.dtype.itemsize for a in args),
+            transcendentals=0,
+        ),
+    )(*args)
+
+
+def wrap(value, size):
+    return jnp.where(value < 0, value + size, jnp.where(value >= size, value - size, value))
+
+
+def pack_kernel(ctx, groups, query, latent, resid, ids, weights, *outs):
+    me = lax.axis_index("ctx")
+    tok, cols = resid.shape[0], resid.shape[1] // ctx
+    rows, width = query.shape
+    parts = rows // tok
+    lane = lax.broadcasted_iota(jnp.int32, (tok, 128), 1)
+    high = jnp.zeros((tok, 128), F32)
+    for k in range(ids.shape[1]):
+        high = high + jnp.where(lane == ids[:, k : k + 1], weights[:, k : k + 1], 0.0)
+    for k in range(ids.shape[1]):
+        high = high + jnp.where(lane == ids[:, k : k + 1] + 64, weights[:, k : k + 1], 0.0)
+    near = high.astype(BF16).astype(F32)
+    routes = jnp.where(lane < 64, near, high - near)
+    extra = (cols + 128) // parts
+    for d, out in enumerate(outs):
+        to = wrap(me + d, ctx)
+        both = jnp.concatenate([lanes(resid, to, cols).astype(F32), routes], axis=1)
+        both = jnp.concatenate([both[:, p * extra : (p + 1) * extra] for p in range(parts)], axis=0)
+        out[:, :width] = query[...]
+        out[:, width : width + extra] = both.astype(BF16)
+        out[:, width + extra :] = latent[...]
+
+
+def attention_kernel(ctx, groups, heads, extra, *refs):
+    pieces, (w_uk, w_uv, w_o), outs, part_ref = (
+        refs[:ctx],
+        refs[ctx : ctx + 3],
+        refs[ctx + 3 : -1],
+        refs[-1],
+    )
+    me, mine = lax.axis_index("ctx"), lax.axis_index(EH)
+    rows = pieces[0].shape[0]
+    width = NOPE + ROPE
+    scale = 1.0 / math.sqrt(width)
+    first = heads * width + extra
+    latent = jnp.concatenate([p[:, first : first + LATENT] for p in pieces], axis=0)
+    rope_keys = jnp.concatenate([p[:, first + LATENT :] for p in pieces], axis=0)
+    query = jnp.concatenate([p[:, : heads * width] for p in pieces], axis=0)
+    keys = jnp.dot(latent, w_uk[...], preferred_element_type=F32).astype(BF16)
+    values = jnp.dot(latent, w_uv[...], preferred_element_type=F32).astype(BF16)
+    total = ctx * rows
+
+    def place(dim):
+        at = lax.broadcasted_iota(jnp.int32, (total, total), dim)
+        block = jnp.zeros_like(at)
+        for d in range(ctx):
+            here = (at >= d * rows) & (at < (d + 1) * rows)
+            block = jnp.where(here, wrap(me - d, ctx) * rows - d * rows, block)
+        return at + block
+
+    allowed = place(1) <= place(0)
+    contract = (((1,), (1,)), ((), ()))
+    done = []
+    for h in range(heads):
+        q = query[:, h * width : (h + 1) * width]
+        k = jnp.concatenate([keys[:, h * NOPE : (h + 1) * NOPE], rope_keys], axis=1)
+        scores = lax.dot_general(q, k, contract, preferred_element_type=F32) * scale
+        scores = jnp.where(allowed, scores, -1e30)
+        exponent = jnp.exp(scores - jnp.max(scores, axis=1, keepdims=True))
+        exponent = jnp.where(allowed, exponent, 0.0)
+        weight = jnp.sum(exponent, axis=1, keepdims=True)
+        summed = jnp.dot(
+            exponent.astype(BF16), values[:, h * NOPE : (h + 1) * NOPE], preferred_element_type=F32
+        )
+        done.append((summed / weight).astype(BF16))
+    partial = jnp.dot(jnp.concatenate(done, axis=1), w_o[...], preferred_element_type=F32)
+    tok = rows // groups
+    for n in range(ctx * groups):
+        part_ref[n] = partial[n * tok : (n + 1) * tok]
+    for s, out in enumerate(outs):
+        to = jnp.bitwise_xor(mine, s)
+        out[...] = jnp.concatenate([part_ref[d * groups + to] for d in range(ctx)], axis=0).astype(
+            BF16
+        )
+
+
+def residual_kernel(ctx, groups, first, extra, *refs):
+    sums, pieces, (travelling, kept, routes) = refs[:groups], refs[groups : groups + ctx], refs[-3:]
+    me = lax.axis_index("ctx")
+    tok, cols = kept.shape[1:]
+    total = sums[0][...].astype(F32)
+    for part in sums[1:]:
+        total = total + part[...].astype(F32)
+    for d in range(ctx):
+        both = pieces[d][:, first : first + extra].astype(F32)
+        both = jnp.concatenate(
+            [both[p * tok : (p + 1) * tok] for p in range(both.shape[0] // tok)], axis=1
+        )
+        at = wrap(me - d, ctx)
+        kept[at] = total[d * tok : (d + 1) * tok] + both[:, :cols]
+        routes[at] = both[:, cols:]
+    travelling[...] = jnp.concatenate([kept[b] for b in range(ctx)], axis=0).astype(BF16)
+
+
+def norm_kernel(ctx, *refs):
+    columns, gain, out = refs[:ctx], refs[ctx], refs[ctx + 1]
+    me = lax.axis_index("ctx")
+    cols = columns[0].shape[1]
+    values = [c[...].astype(F32) for c in columns]
+    squares = values[0] * values[0]
+    for v in values[1:]:
+        squares = squares + v * v
+    mean = jnp.sum(squares, axis=1, keepdims=True) * (1.0 / out.shape[1])
+    inverse = lax.rsqrt(mean + 1e-06)
+    for d, v in enumerate(values):
+        at = pl.ds(pl.multiple_of(wrap(me - d, ctx) * cols, 128), cols)
+        out[:, at] = (v * inverse * gain[:, at]).astype(BF16)
+
+
+def hidden_kernel(near, far, w_gate, w_up, out):
+    rows = jnp.concatenate([near[...], far[...]], axis=0)
+    gate_part = jnp.dot(rows, w_gate[0], preferred_element_type=F32)
+    up_part = jnp.dot(rows, w_up[0], preferred_element_type=F32)
+    out[...] = (gate_part / (1.0 + jnp.exp(-gate_part)) * up_part).astype(BF16)
+
+
+def down_kernel(ctx, *refs):
+    hidden, w_down, outs = refs[:ctx], refs[ctx], refs[ctx + 1 :]
+    me = lax.axis_index("ctx")
+    ff = hidden[0].shape[1]
+    total = 0.0
+    for d in range(ctx):
+        at = pl.ds(pl.multiple_of(wrap(me - d, ctx) * ff, ff), ff)
+        total = total + jnp.dot(hidden[d][...], w_down[0, at, :], preferred_element_type=F32)
+    rows = outs[0].shape[0]
+    for n, out in enumerate(outs):
+        out[...] = total[n * rows : (n + 1) * rows].astype(BF16)
+
+
+def combine_kernel(ctx, groups, *refs):
+    parts, kept, routes, outs = refs[:groups], refs[groups], refs[groups + 1], refs[groups + 2 : -1]
+    final = refs[-1]
+    me, mine = lax.axis_index("ctx"), lax.axis_index(EH)
+    tok, cols = kept.shape[1:]
+    weights = jnp.concatenate([routes[b] for b in range(ctx)], axis=0)
+    total = jnp.concatenate([kept[b] for b in range(ctx)], axis=0)
+    lane = lax.broadcasted_iota(jnp.int32, weights.shape, 1)
+    for s, part in enumerate(parts):
+        expert = jnp.bitwise_xor(mine, s)
+        here = (lane == expert) | (lane == expert + 64)
+        weight = jnp.sum(jnp.where(here, weights, 0.0), axis=1, keepdims=True)
+        total = total + part[...].astype(F32) * weight
+    for b in range(ctx):
+        final[b] = total[b * tok : (b + 1) * tok]
+    for d, out in enumerate(outs):
+        out[...] = final[wrap(me + d, ctx)].astype(BF16)
+
+
+def gather_kernel(ctx, *refs):
+    parts, out = refs[:ctx], refs[ctx]
+    me = lax.axis_index("ctx")
+    cols = parts[0].shape[1]
+    for d, part in enumerate(parts):
+        out[:, pl.ds(pl.multiple_of(wrap(me - d, ctx) * cols, 128), cols)] = part[...]
+
+
+def swap(value, step):
+    size = lax.axis_size(EH)
+    return lax.ppermute(value, EH, [(i, i ^ step) for i in range(size)])
+
+
+def around(value, ctx):
+    return [value] + [send(value, "ctx", d) for d in range(1, ctx)]
+
+
+def fast_shards(
+    latent, query, w_uk, w_uv, w_o, resid, norm_gain, w_gate, w_up, w_down, expert_ids, route_weights
+):
+    ctx, groups = lax.axis_size("ctx"), lax.axis_size(EH)
+    rows, width = query.shape
+    heads = width // (NOPE + ROPE)
+    tok, model = resid.shape
+    cols = w_o.shape[1]
+    ff = w_gate.shape[2]
+    extra = (cols + 128) * tok // rows
+    here = ctx * tok
+    like = jax.ShapeDtypeStruct
+
+    packed = like((rows, width + extra + latent.shape[1]), BF16)
+    packs = call(
+        functools.partial(pack_kernel, ctx, groups),
+        [packed] * ctx,
+        [query, latent, resid, expert_ids, route_weights],
+        0,
+        8,
+    )
+    pieces = [packs[0]] + [send(packs[d], "ctx", d) for d in range(1, ctx)]
+    partial = pl.pallas_call(
+        functools.partial(attention_kernel, ctx, groups, heads, extra),
+        out_shape=[like((here, cols), BF16)] * groups,
+        in_specs=[pl.BlockSpec(memory_space=pltpu.VMEM)] * (ctx + 3),
+        out_specs=[pl.BlockSpec(memory_space=pltpu.VMEM)] * groups,
+        scratch_shapes=[pltpu.VMEM((ctx * groups, tok, cols), F32)],
+        compiler_params=pltpu.CompilerParams(vmem_limit_bytes=16 << 20),
+        cost_estimate=pl.CostEstimate(
+            flops=2 * ctx * rows * heads * NOPE * (2 * LATENT + cols),
+            bytes_accessed=4 << 20,
+            transcendentals=heads * (ctx * rows) ** 2,
+        ),
+    )(*pieces, w_uk, w_uv, w_o)
+    sums = [partial[0]] + [swap(partial[s], s) for s in range(1, groups)]
+    travelling, kept, routes = call(
+        functools.partial(residual_kernel, ctx, groups, width, extra),
+        [like((here, cols), BF16), like((ctx, tok, cols), F32), like((ctx, tok, 128), F32)],
+        sums + pieces,
+        0,
+        8,
+    )
+    mine = call(
+        functools.partial(norm_kernel, ctx),
+        like((here, model), BF16),
+        around(travelling, ctx) + [norm_gain.reshape(1, model)],
+        0,
+        8,
+    )
+    work = 4 * 2 * here * model * ff
+    sibling, other = swap(mine, 1), swap(mine, groups // 2)
+    hidden = call(
+        hidden_kernel, like((2 * here, ff), BF16), [mine, sibling, w_gate, w_up], work, 16
+    )
+    near = around(hidden, ctx)
+    other_sibling = swap(other, 1)
+    hidden = call(
+        hidden_kernel, like((2 * here, ff), BF16), [other, other_sibling, w_gate, w_up], work, 16
+    )
+    far = around(hidden, ctx)
+    down = functools.partial(down_kernel, ctx)
+    pair = [like((here, cols), BF16)] * 2
+    near = call(down, pair, near + [w_down], work // 2, 16)
+    far = call(down, pair, far + [w_down], work // 2, 16)
+    parts = [near[0], swap(near[1], 1), swap(far[0], groups // 2), swap(far[1], groups // 2 + 1)]
+    finals = pl.pallas_call(
+        functools.partial(combine_kernel, ctx, groups),
+        out_shape=[like((tok, cols), BF16)] * ctx,
+        in_specs=[pl.BlockSpec(memory_space=pltpu.VMEM)] * (groups + 2),
+        out_specs=[pl.BlockSpec(memory_space=pltpu.VMEM)] * ctx,
+        scratch_shapes=[pltpu.VMEM((ctx, tok, cols), F32)],
+        compiler_params=pltpu.CompilerParams(vmem_limit_bytes=8 << 20),
+    )(*parts, kept, routes)
+    return call(
+        functools.partial(gather_kernel, ctx),
+        like((tok, model), BF16),
+        [finals[0]] + [send(finals[d], "ctx", d) for d in range(1, ctx)],
+        0,
+        8,
+    )
+
+
 def solution(mesh):
     placed = (
         P(("groups", "ctx"), None),
@@ -168,8 +441,17 @@
         P(("groups", "ctx", "exp", "head"), None),
         P(("groups", "ctx", "exp", "head"), None),
     )
+    experts = mesh.shape["exp"] * mesh.shape["head"]
+
+    def step(*args):
+        cols, rows = args[4].shape[1], args[1].shape[0]
+        parts = rows // args[5].shape[0]
+        whole = cols % 128 == 0 and (cols + 128) % (128 * parts) == 0 and parts == experts
+        small = rows * mesh.shape["ctx"] <= 256
+        return (fast_shards if experts == 4 and whole and small else shards)(*args)
+
     return jax.shard_map(
-        shards,
+        step,
         mesh=mesh,
         in_specs=placed,
         out_specs=P(("groups", "ctx", "exp", "head"), None),

time: 74.2 us -> 75.8 us (1.022)
  waiting for transfers between devices: 17.4 us -> 28.5 us
  blocking collectives: 9.2 us -> 0 us
  matrix products: 7.51 us -> 0 us
  local copies, waits for them, and re-layouts: 2.77 us -> 9.93 us
  Pallas kernels: 0 us -> 6.41 us
  starting transfers between devices: 35.1 us -> 30.3 us
  other arithmetic: 1.54 us -> 0 us
    ppermute x0 -> x9, waiting for transfers between devices: none -> 13.3 us  [swap(): return lax.ppermute(value, EH, [(i, i ^ step) for i in range(size)])]
    ppermute x24 -> x15, starting transfers between devices: 35.1 us -> 25.6 us  [send(): lax.ppermute(value, axis, [(i, (i + step) % size) for i in range(size)])]
    all_gather x1 -> x0, blocking collectives: 9.2 us -> none  [shards(): everything = lax.all_gather(normalized, EH, axis=0, tiled=True)]
    unnamed x15 -> x20, local copies, waits for them, and re-layouts: 0.92 us -> 9.21 us
    dot_general x18 -> x0, matrix products: 7.51 us -> none  [the longest x1 1.27 us: attend(): keys = jnp.dot(compressed, w_uk, preferred_element_type=F32).astype(BF16)]
    pallas_call x0 -> x10, Pallas kernels: none -> 6.41 us  [the longest x8 5.14 us: call(): pl.pallas_call(kernel, out_shape=out, in_specs=[pl.BlockSpec(memory_space...]
    ppermute x0 -> x9, starting transfers between devices: none -> 4.74 us  [swap(): return lax.ppermute(value, EH, [(i, i ^ step) for i in range(size)])]
    ppermute x24 -> x15, waiting for transfers between devices: 17.4 us -> 15.2 us  [send(): lax.ppermute(value, axis, [(i, (i + step) % size) for i in range(size)])]
  transfers between devices with their start and end apart: 24 -> 24, of which waited for: 8 -> 15; matrix products, arithmetic and copies ran while one was open for 9% -> 1% of each run, Pallas kernels for 0% -> 6%
where the time goes in v2:
time: 75.8 us; the launch traced here: 75.3 us
  starting transfers between devices  30.3 us (40%)
  waiting for transfers between devices  28.5 us (38%)
  local copies, waits for them, and re-layouts  9.93 us (13%)
  Pallas kernels  6.41 us (8%)
    ppermute x15, starting transfers between devices, send(): lax.ppermute(value, axis, [(i, (i + step) % size) for i in range(size)])  25.6 us
    ppermute x15, waiting for transfers between devices, send(): lax.ppermute(value, axis, [(i, (i + step) % size) for i in range(size)])  15.2 us
    ppermute x9, waiting for transfers between devices, swap(): return lax.ppermute(value, EH, [(i, i ^ step) for i in range(size)])  13.3 us
    unnamed x20, local copies, waits for them, and re-layouts  9.21 us
    pallas_call x8, Pallas kernels, call(): pl.pallas_call(kernel, out_shape=out, in_specs=[pl.BlockSpec(memory_space...  5.14 us
    ppermute x9, starting transfers between devices, swap(): return lax.ppermute(value, EH, [(i, i ^ step) for i in range(size)])  4.74 us
  transfers between devices with their start and end apart: 24, of which 15 were waited for; matrix products, arithmetic and copies ran while one was open for 1% of the time, Pallas kernels for 6%

profile of v2, /device:TPU:0, one launch (start us, length us, event | category | flops | bytes accessed | tf_op | source)
XLA Modules:
  0.0 75.3 jit_solution(12078284974227595083)
XLA Ops:
  4.0 3.1 %collective-permute-start = (bf16[32,1600]{1,0:T(8,128)(2,1)S(1)}, bf16[32,1600]{1,0:T(8,128)(2,1)S(1)}, u32[]{:S(2)}, u32[]{:S(2)}) collective-permute-start(bf16[32,1600]{1,0:T(8,128)(2,1)S(1)} %get-tuple-element.25), channel_id=1, source_target_pairs={{0,4},{4,8},{8,12},{12,0},{1,5},{5,9},{9,13},{13,1},{2,6},{6,10},{... | collective-permute-start | bytes 307208 | tf_op jit(solution)/shard_map/ppermute | solution.py:21
  7.1 2.6 %collective-permute-start.1 = (bf16[32,1600]{1,0:T(8,128)(2,1)S(1)}, bf16[32,1600]{1,0:T(8,128)(2,1)S(1)}, u32[]{:S(2)}, u32[]{:S(2)}) collective-permute-start(bf16[32,1600]{1,0:T(8,128)(2,1)S(1)} %get-tuple-element.26), channel_id=1, source_target_pairs={{0,8},{4,12},{8,0},{12,4},{1,9},{5,13},{9,1},{13,5},{2,10},{6,14},... | collective-permute-start | bytes 307208 | tf_op jit(solution)/shard_map/ppermute | solution.py:21
  9.7 1.3 %collective-permute-start.2 = (bf16[32,1600]{1,0:T(8,128)(2,1)S(1)}, bf16[32,1600]{1,0:T(8,128)(2,1)S(1)}, u32[]{:S(2)}, u32[]{:S(2)}) collective-permute-start(bf16[32,1600]{1,0:T(8,128)(2,1)S(1)} %get-tuple-element.27), channel_id=1, source_target_pairs={{0,12},{4,0},{8,4},{12,8},{1,13},{5,1},{9,5},{13,9},{2,14},{6,2},{... | collective-permute-start | bytes 307208 | tf_op jit(solution)/shard_map/ppermute | solution.py:21
  11.0 2.0 %collective-permute-done.refs_1_.refs_5_ = bf16[32,1600]{1,0:T(8,128)(2,1)S(1)} collective-permute-done((bf16[32,1600]{1,0:T(8,128)(2,1)S(1)}, bf16[32,1600]{1,0:T(8,128)(2,1)S(1)}, u32[]{:S(2)}, u32[]{:S(2)}) %collective-permute-start) | collective-permute-done | bytes 102432 | tf_op jit(solution)/shard_map/ppermute | solution.py:21
  13.0 3.8 %collective-permute-done.1.refs_2_.refs_6_ = bf16[32,1600]{1,0:T(8,128)(2,1)S(1)} collective-permute-done((bf16[32,1600]{1,0:T(8,128)(2,1)S(1)}, bf16[32,1600]{1,0:T(8,128)(2,1)S(1)}, u32[]{:S(2)}, u32[]{:S(2)}) %collective-permute-start.1) | collective-permute-done | bytes 102432 | tf_op jit(solution)/shard_map/ppermute | solution.py:21
  21.3 1.6 %collective-permute-start.4 = (bf16[32,896]{1,0:T(8,128)(2,1)S(1)}, bf16[32,896]{1,0:T(8,128)(2,1)S(1)}, u32[]{:S(2)}, u32[]{:S(2)}) collective-permute-start(bf16[32,896]{1,0:T(8,128)(2,1)S(1)} %get-tuple-element.30), channel_id=1, source_target_pairs={{0,2},{1,3},{2,0},{3,1},{4,6},{5,7},{6,4},{7,5},{8,10},{9,11},{10,... | collective-permute-start | bytes 172040 | tf_op jit(solution)/shard_map/ppermute | solution.py:339
  23.1 2.5 %collective-permute-done.4.refs_2_ = bf16[32,896]{1,0:T(8,128)(2,1)S(1)} collective-permute-done((bf16[32,896]{1,0:T(8,128)(2,1)S(1)}, bf16[32,896]{1,0:T(8,128)(2,1)S(1)}, u32[]{:S(2)}, u32[]{:S(2)}) %collective-permute-start.4) | collective-permute-done | bytes 57376 | tf_op jit(solution)/shard_map/ppermute | solution.py:339
  26.7 2.8 %collective-permute-start.6 = (bf16[32,896]{1,0:T(8,128)(2,1)S(1)}, bf16[32,896]{1,0:T(8,128)(2,1)S(1)}, u32[]{:S(2)}, u32[]{:S(2)}) collective-permute-start(bf16[32,896]{1,0:T(8,128)(2,1)S(1)} %get-tuple-element.32.refs_0_), channel_id=1, source_target_pairs={{0,4},{4,8},{8,12},{12,0},{1,5},{5,9},{9,13},{13,1},{2,6},{6,10},{... | collective-permute-start | bytes 172040 | tf_op jit(solution)/shard_map/ppermute | solution.py:21
  29.5 1.6 %collective-permute-start.7 = (bf16[32,896]{1,0:T(8,128)(2,1)S(1)}, bf16[32,896]{1,0:T(8,128)(2,1)S(1)}, u32[]{:S(2)}, u32[]{:S(2)}) collective-permute-start(bf16[32,896]{1,0:T(8,128)(2,1)S(1)} %get-tuple-element.32.refs_0_), channel_id=1, source_target_pairs={{0,8},{4,12},{8,0},{12,4},{1,9},{5,13},{9,1},{13,5},{2,10},{6,14},... | collective-permute-start | bytes 172040 | tf_op jit(solution)/shard_map/ppermute | solution.py:21
  33.0 2.4 %collective-permute-done.7.refs_2_ = bf16[32,896]{1,0:T(8,128)(2,1)S(1)} collective-permute-done((bf16[32,896]{1,0:T(8,128)(2,1)S(1)}, bf16[32,896]{1,0:T(8,128)(2,1)S(1)}, u32[]{:S(2)}, u32[]{:S(2)}) %collective-permute-start.7) | collective-permute-done | bytes 57376 | tf_op jit(solution)/shard_map/ppermute | solution.py:21
  36.0 1.3 %collective-permute-start.14 = (bf16[32,3584]{1,0:T(8,128)(2,1)S(1)}, bf16[32,3584]{1,0:T(8,128)(2,1)S(1)}, u32[]{:S(2)}, u32[]{:S(2)}) collective-permute-start(bf16[32,3584]{1,0:T(8,128)(2,1)S(1)} %shard_map.121.near), channel_id=1, source_target_pairs={{0,2},{1,3},{2,0},{3,1},{4,6},{5,7},{6,4},{7,5},{8,10},{9,11},{10,... | collective-permute-start | bytes 688136 | tf_op jit(solution)/shard_map/ppermute | solution.py:339
  37.4 5.6 %collective-permute-done.14.near = bf16[32,3584]{1,0:T(8,128)(2,1)S(1)} collective-permute-done((bf16[32,3584]{1,0:T(8,128)(2,1)S(1)}, bf16[32,3584]{1,0:T(8,128)(2,1)S(1)}, u32[]{:S(2)}, u32[]{:S(2)}) %collective-permute-start.14) | collective-permute-done | bytes 229408 | tf_op jit(solution)/shard_map/ppermute | solution.py:339
  43.1 2.0 %copy-done.1 = bf16[1,3584,512]{2,1,0:T(8,128)(2,1)S(1)} copy-done((bf16[1,3584,512]{2,1,0:T(8,128)(2,1)S(1)}, bf16[1,3584,512]{2,1,0:T(8,128)(2,1)}, u32[]{:S(2)}) %copy-start.1) | copy-done | bytes 3670040
  45.1 1.4 %shard_map.122.refs_0_ = bf16[64,512]{1,0:T(8,128)(2,1)S(1)} custom-call(bf16[32,3584]{1,0:T(8,128)(2,1)S(1)} %shard_map.121.near, bf16[32,3584]{1,0:T(8,128)(2,1)S(1)} %collective-permute-done.9.far, bf16[1,3584,512]{2,1,0:T(8,128)(2,1)S(1)} %copy-done, bf16[1,3584,512]{2,1,0:T(8,128)(2,1)S(1)} %copy-done.1), custom_call_target="tpu_custom_call" | custom-call | flops 469762048 | bytes 7798784 | tf_op jit(solution)/shard_map/pallas_call | solution.py:164
  46.5 1.8 %collective-permute-start.10 = (bf16[64,512]{1,0:T(8,128)(2,1)S(1)}, bf16[64,512]{1,0:T(8,128)(2,1)S(1)}, u32[]{:S(2)}, u32[]{:S(2)}) collective-permute-start(bf16[64,512]{1,0:T(8,128)(2,1)S(1)} %shard_map.122.refs_0_), channel_id=1, source_target_pairs={{0,4},{4,8},{8,12},{12,0},{1,5},{5,9},{9,13},{13,1},{2,6},{6,10},{... | collective-permute-start | bytes 196616 | tf_op jit(solution)/shard_map/ppermute | solution.py:21
  48.9 1.9 %collective-permute-start.12 = (bf16[64,512]{1,0:T(8,128)(2,1)S(1)}, bf16[64,512]{1,0:T(8,128)(2,1)S(1)}, u32[]{:S(2)}, u32[]{:S(2)}) collective-permute-start(bf16[64,512]{1,0:T(8,128)(2,1)S(1)} %shard_map.122.refs_0_), channel_id=1, source_target_pairs={{0,12},{4,0},{8,4},{12,8},{1,13},{5,1},{9,5},{13,9},{2,14},{6,2},{... | collective-permute-start | bytes 196616 | tf_op jit(solution)/shard_map/ppermute | solution.py:21
  50.8 1.4 %shard_map.124.refs_0_ = bf16[64,512]{1,0:T(8,128)(2,1)S(1)} custom-call(bf16[32,3584]{1,0:T(8,128)(2,1)S(1)} %collective-permute-done.14.near, bf16[32,3584]{1,0:T(8,128)(2,1)S(1)} %collective-permute-done.15.far, bf16[1,3584,512]{2,1,0:T(8,128)(2,1)S(1)} %copy-done, bf16[1,3584,512]{2,1,0:T(8,128)(2,1)S(1)} %copy-done.1), custom_call_target="tpu_custom_call" | custom-call | flops 469762048 | bytes 7798784 | tf_op jit(solution)/shard_map/pallas_call | solution.py:164
  52.4 2.3 %collective-permute-start.17 = (bf16[64,512]{1,0:T(8,128)(2,1)S(1)}, bf16[64,512]{1,0:T(8,128)(2,1)S(1)}, u32[]{:S(2)}, u32[]{:S(2)}) collective-permute-start(bf16[64,512]{1,0:T(8,128)(2,1)S(1)} %shard_map.124.refs_0_), channel_id=1, source_target_pairs={{0,8},{4,12},{8,0},{12,4},{1,9},{5,13},{9,1},{13,5},{2,10},{6,14},... | collective-permute-start | bytes 196616 | tf_op jit(solution)/shard_map/ppermute | solution.py:21
  54.7 2.0 %collective-permute-start.18 = (bf16[64,512]{1,0:T(8,128)(2,1)S(1)}, bf16[64,512]{1,0:T(8,128)(2,1)S(1)}, u32[]{:S(2)}, u32[]{:S(2)}) collective-permute-start(bf16[64,512]{1,0:T(8,128)(2,1)S(1)} %shard_map.124.refs_0_), channel_id=1, source_target_pairs={{0,12},{4,0},{8,4},{12,8},{1,13},{5,1},{9,5},{13,9},{2,14},{6,2},{... | collective-permute-start | bytes 196616 | tf_op jit(solution)/shard_map/ppermute | solution.py:21
  57.6 1.4 %collective-permute-done.16.refs_1_ = bf16[64,512]{1,0:T(8,128)(2,1)S(1)} collective-permute-done((bf16[64,512]{1,0:T(8,128)(2,1)S(1)}, bf16[64,512]{1,0:T(8,128)(2,1)S(1)}, u32[]{:S(2)}, u32[]{:S(2)}) %collective-permute-start.16) | collective-permute-done | bytes 65568 | tf_op jit(solution)/shard_map/ppermute | solution.py:21
  59.0 2.4 %collective-permute-done.17.refs_2_ = bf16[64,512]{1,0:T(8,128)(2,1)S(1)} collective-permute-done((bf16[64,512]{1,0:T(8,128)(2,1)S(1)}, bf16[64,512]{1,0:T(8,128)(2,1)S(1)}, u32[]{:S(2)}, u32[]{:S(2)}) %collective-permute-start.17) | collective-permute-done | bytes 65568 | tf_op jit(solution)/shard_map/ppermute | solution.py:21
  62.1 1.3 %collective-permute-start.19 = (bf16[32,896]{1,0:T(8,128)(2,1)S(1)}, bf16[32,896]{1,0:T(8,128)(2,1)S(1)}, u32[]{:S(2)}, u32[]{:S(2)}) collective-permute-start(bf16[32,896]{1,0:T(8,128)(2,1)S(1)} %get-tuple-element.35), channel_id=1, source_target_pairs={{0,2},{1,3},{2,0},{3,1},{4,6},{5,7},{6,4},{7,5},{8,10},{9,11},{10,... | collective-permute-start | bytes 172040 | tf_op jit(solution)/shard_map/ppermute | solution.py:339
  63.5 2.8 %collective-permute-done.19.refs_2_ = bf16[32,896]{1,0:T(8,128)(2,1)S(1)} collective-permute-done((bf16[32,896]{1,0:T(8,128)(2,1)S(1)}, bf16[32,896]{1,0:T(8,128)(2,1)S(1)}, u32[]{:S(2)}, u32[]{:S(2)}) %collective-permute-start.19) | collective-permute-done | bytes 57376 | tf_op jit(solution)/shard_map/ppermute | solution.py:339
  67.7 2.0 %collective-permute-start.21 = (bf16[8,896]{1,0:T(8,128)(2,1)S(1)}, bf16[8,896]{1,0:T(8,128)(2,1)S(1)}, u32[]{:S(2)}, u32[]{:S(2)}) collective-permute-start(bf16[8,896]{1,0:T(8,128)(2,1)S(1)} %get-tuple-element.40), channel_id=1, source_target_pairs={{0,4},{4,8},{8,12},{12,0},{1,5},{5,9},{9,13},{13,1},{2,6},{6,10},{... | collective-permute-start | bytes 43016 | tf_op jit(solution)/shard_map/ppermute | solution.py:21
  (55 shorter events, 21.8 us)
Async XLA Ops:
  4.0 9.0 %collective-permute-start = (bf16[32,1600]{1,0:T(8,128)(2,1)S(1)}, bf16[32,1600]{1,0:T(8,128)(2,1)S(1)}, u32[]{:S(2)}, u32[]{:S(2)}) collective-permute-start(bf16[32,1600]{1,0:T(8,128)(2,1)S(1)} %get-tuple-element.25), channel_id=1, source_target_pairs={{0,4},{4,8},{8,12},{12,0},{1,5},{5,9},{9,13},{13,1},{2,6},{6,10},{... | collective-permute-start | bytes 307208 | tf_op jit(solution)/shard_map/ppermute | solution.py:21
  7.1 9.7 %collective-permute-start.1 = (bf16[32,1600]{1,0:T(8,128)(2,1)S(1)}, bf16[32,1600]{1,0:T(8,128)(2,1)S(1)}, u32[]{:S(2)}, u32[]{:S(2)}) collective-permute-start(bf16[32,1600]{1,0:T(8,128)(2,1)S(1)} %get-tuple-element.26), channel_id=1, source_target_pairs={{0,8},{4,12},{8,0},{12,4},{1,9},{5,13},{9,1},{13,5},{2,10},{6,14},... | collective-permute-start | bytes 307208 | tf_op jit(solution)/shard_map/ppermute | solution.py:21
  9.7 7.1 %collective-permute-start.2 = (bf16[32,1600]{1,0:T(8,128)(2,1)S(1)}, bf16[32,1600]{1,0:T(8,128)(2,1)S(1)}, u32[]{:S(2)}, u32[]{:S(2)}) collective-permute-start(bf16[32,1600]{1,0:T(8,128)(2,1)S(1)} %get-tuple-element.27), channel_id=1, source_target_pairs={{0,12},{4,0},{8,4},{12,8},{1,13},{5,1},{9,5},{13,9},{2,14},{6,2},{... | collective-permute-start | bytes 307208 | tf_op jit(solution)/shard_map/ppermute | solution.py:21
  21.2 1.9 %collective-permute-start.3 = (bf16[32,896]{1,0:T(8,128)(2,1)S(1)}, bf16[32,896]{1,0:T(8,128)(2,1)S(1)}, u32[]{:S(2)}, u32[]{:S(2)}) collective-permute-start(bf16[32,896]{1,0:T(8,128)(2,1)S(1)} %get-tuple-element.29), channel_id=1, source_target_pairs={{0,1},{1,0},{2,3},{3,2},{4,5},{5,4},{6,7},{7,6},{8,9},{9,8},{10,11... | collective-permute-start | bytes 172040 | tf_op jit(solution)/shard_map/ppermute | solution.py:339
  21.3 4.3 %collective-permute-start.4 = (bf16[32,896]{1,0:T(8,128)(2,1)S(1)}, bf16[32,896]{1,0:T(8,128)(2,1)S(1)}, u32[]{:S(2)}, u32[]{:S(2)}) collective-permute-start(bf16[32,896]{1,0:T(8,128)(2,1)S(1)} %get-tuple-element.30), channel_id=1, source_target_pairs={{0,2},{1,3},{2,0},{3,1},{4,6},{5,7},{6,4},{7,5},{8,10},{9,11},{10,... | collective-permute-start | bytes 172040 | tf_op jit(solution)/shard_map/ppermute | solution.py:339
  22.8 3.9 %collective-permute-start.5 = (bf16[32,896]{1,0:T(8,128)(2,1)S(1)}, bf16[32,896]{1,0:T(8,128)(2,1)S(1)}, u32[]{:S(2)}, u32[]{:S(2)}) collective-permute-start(bf16[32,896]{1,0:T(8,128)(2,1)S(1)} %get-tuple-element.31), channel_id=1, source_target_pairs={{0,3},{1,2},{2,1},{3,0},{4,7},{5,6},{6,5},{7,4},{8,11},{9,10},{10,... | collective-permute-start | bytes 172040 | tf_op jit(solution)/shard_map/ppermute | solution.py:339
  26.7 6.2 %collective-permute-start.6 = (bf16[32,896]{1,0:T(8,128)(2,1)S(1)}, bf16[32,896]{1,0:T(8,128)(2,1)S(1)}, u32[]{:S(2)}, u32[]{:S(2)}) collective-permute-start(bf16[32,896]{1,0:T(8,128)(2,1)S(1)} %get-tuple-element.32.refs_0_), channel_id=1, source_target_pairs={{0,4},{4,8},{8,12},{12,0},{1,5},{5,9},{9,13},{13,1},{2,6},{6,10},{... | collective-permute-start | bytes 172040 | tf_op jit(solution)/shard_map/ppermute | solution.py:21
  29.5 5.8 %collective-permute-start.7 = (bf16[32,896]{1,0:T(8,128)(2,1)S(1)}, bf16[32,896]{1,0:T(8,128)(2,1)S(1)}, u32[]{:S(2)}, u32[]{:S(2)}) collective-permute-start(bf16[32,896]{1,0:T(8,128)(2,1)S(1)} %get-tuple-element.32.refs_0_), channel_id=1, source_target_pairs={{0,8},{4,12},{8,0},{12,4},{1,9},{5,13},{9,1},{13,5},{2,10},{6,14},... | collective-permute-start | bytes 172040 | tf_op jit(solution)/shard_map/ppermute | solution.py:21
  31.1 4.8 %collective-permute-start.8 = (bf16[32,896]{1,0:T(8,128)(2,1)S(1)}, bf16[32,896]{1,0:T(8,128)(2,1)S(1)}, u32[]{:S(2)}, u32[]{:S(2)}) collective-permute-start(bf16[32,896]{1,0:T(8,128)(2,1)S(1)} %get-tuple-element.32.refs_0_), channel_id=1, source_target_pairs={{0,12},{4,0},{8,4},{12,8},{1,13},{5,1},{9,5},{13,9},{2,14},{6,2},{... | collective-permute-start | bytes 172040 | tf_op jit(solution)/shard_map/ppermute | solution.py:21
  36.0 7.0 %collective-permute-start.14 = (bf16[32,3584]{1,0:T(8,128)(2,1)S(1)}, bf16[32,3584]{1,0:T(8,128)(2,1)S(1)}, u32[]{:S(2)}, u32[]{:S(2)}) collective-permute-start(bf16[32,3584]{1,0:T(8,128)(2,1)S(1)} %shard_map.121.near), channel_id=1, source_target_pairs={{0,2},{1,3},{2,0},{3,1},{4,6},{5,7},{6,4},{7,5},{8,10},{9,11},{10,... | collective-permute-start | bytes 688136 | tf_op jit(solution)/shard_map/ppermute | solution.py:339
  37.4 5.6 %collective-permute-start.9 = (bf16[32,3584]{1,0:T(8,128)(2,1)S(1)}, bf16[32,3584]{1,0:T(8,128)(2,1)S(1)}, u32[]{:S(2)}, u32[]{:S(2)}) collective-permute-start(bf16[32,3584]{1,0:T(8,128)(2,1)S(1)} %shard_map.121.near), channel_id=1, source_target_pairs={{0,1},{1,0},{2,3},{3,2},{4,5},{5,4},{6,7},{7,6},{8,9},{9,8},{10,11... | collective-permute-start | bytes 688136 | tf_op jit(solution)/shard_map/ppermute | solution.py:339
  43.0 7.7 %collective-permute-start.15 = (bf16[32,3584]{1,0:T(8,128)(2,1)S(1)}, bf16[32,3584]{1,0:T(8,128)(2,1)S(1)}, u32[]{:S(2)}, u32[]{:S(2)}) collective-permute-start(bf16[32,3584]{1,0:T(8,128)(2,1)S(1)} %collective-permute-done.14.near), channel_id=1, source_target_pairs={{0,1},{1,0},{2,3},{3,2},{4,5},{5,4},{6,7},{7,6},{8,9},{9,8},{10,11... | collective-permute-start | bytes 688136 | tf_op jit(solution)/shard_map/ppermute | solution.py:339
  46.5 8.2 %collective-permute-start.10 = (bf16[64,512]{1,0:T(8,128)(2,1)S(1)}, bf16[64,512]{1,0:T(8,128)(2,1)S(1)}, u32[]{:S(2)}, u32[]{:S(2)}) collective-permute-start(bf16[64,512]{1,0:T(8,128)(2,1)S(1)} %shard_map.122.refs_0_), channel_id=1, source_target_pairs={{0,4},{4,8},{8,12},{12,0},{1,5},{5,9},{9,13},{13,1},{2,6},{6,10},{... | collective-permute-start | bytes 196616 | tf_op jit(solution)/shard_map/ppermute | solution.py:21
  48.3 8.4 %collective-permute-start.11 = (bf16[64,512]{1,0:T(8,128)(2,1)S(1)}, bf16[64,512]{1,0:T(8,128)(2,1)S(1)}, u32[]{:S(2)}, u32[]{:S(2)}) collective-permute-start(bf16[64,512]{1,0:T(8,128)(2,1)S(1)} %shard_map.122.refs_0_), channel_id=1, source_target_pairs={{0,8},{4,12},{8,0},{12,4},{1,9},{5,13},{9,1},{13,5},{2,10},{6,14},... | collective-permute-start | bytes 196616 | tf_op jit(solution)/shard_map/ppermute | solution.py:21
  48.9 7.9 %collective-permute-start.12 = (bf16[64,512]{1,0:T(8,128)(2,1)S(1)}, bf16[64,512]{1,0:T(8,128)(2,1)S(1)}, u32[]{:S(2)}, u32[]{:S(2)}) collective-permute-start(bf16[64,512]{1,0:T(8,128)(2,1)S(1)} %shard_map.122.refs_0_), channel_id=1, source_target_pairs={{0,12},{4,0},{8,4},{12,8},{1,13},{5,1},{9,5},{13,9},{2,14},{6,2},{... | collective-permute-start | bytes 196616 | tf_op jit(solution)/shard_map/ppermute | solution.py:21
  52.1 6.8 %collective-permute-start.16 = (bf16[64,512]{1,0:T(8,128)(2,1)S(1)}, bf16[64,512]{1,0:T(8,128)(2,1)S(1)}, u32[]{:S(2)}, u32[]{:S(2)}) collective-permute-start(bf16[64,512]{1,0:T(8,128)(2,1)S(1)} %shard_map.124.refs_0_), channel_id=1, source_target_pairs={{0,4},{4,8},{8,12},{12,0},{1,5},{5,9},{9,13},{13,1},{2,6},{6,10},{... | collective-permute-start | bytes 196616 | tf_op jit(solution)/shard_map/ppermute | solution.py:21
  52.4 9.0 %collective-permute-start.17 = (bf16[64,512]{1,0:T(8,128)(2,1)S(1)}, bf16[64,512]{1,0:T(8,128)(2,1)S(1)}, u32[]{:S(2)}, u32[]{:S(2)}) collective-permute-start(bf16[64,512]{1,0:T(8,128)(2,1)S(1)} %shard_map.124.refs_0_), channel_id=1, source_target_pairs={{0,8},{4,12},{8,0},{12,4},{1,9},{5,13},{9,1},{13,5},{2,10},{6,14},... | collective-permute-start | bytes 196616 | tf_op jit(solution)/shard_map/ppermute | solution.py:21
  54.7 6.6 %collective-permute-start.18 = (bf16[64,512]{1,0:T(8,128)(2,1)S(1)}, bf16[64,512]{1,0:T(8,128)(2,1)S(1)}, u32[]{:S(2)}, u32[]{:S(2)}) collective-permute-start(bf16[64,512]{1,0:T(8,128)(2,1)S(1)} %shard_map.124.refs_0_), channel_id=1, source_target_pairs={{0,12},{4,0},{8,4},{12,8},{1,13},{5,1},{9,5},{13,9},{2,14},{6,2},{... | collective-permute-start | bytes 196616 | tf_op jit(solution)/shard_map/ppermute | solution.py:21
  57.5 5.9 %collective-permute-start.13 = (bf16[32,896]{1,0:T(8,128)(2,1)S(1)}, bf16[32,896]{1,0:T(8,128)(2,1)S(1)}, u32[]{:S(2)}, u32[]{:S(2)}) collective-permute-start(bf16[32,896]{1,0:T(8,128)(2,1)S(1)} %get-tuple-element.34), channel_id=1, source_target_pairs={{0,1},{1,0},{2,3},{3,2},{4,5},{5,4},{6,7},{7,6},{8,9},{9,8},{10,11... | collective-permute-start | bytes 172040 | tf_op jit(solution)/shard_map/ppermute | solution.py:339
  62.1 4.2 %collective-permute-start.19 = (bf16[32,896]{1,0:T(8,128)(2,1)S(1)}, bf16[32,896]{1,0:T(8,128)(2,1)S(1)}, u32[]{:S(2)}, u32[]{:S(2)}) collective-permute-start(bf16[32,896]{1,0:T(8,128)(2,1)S(1)} %get-tuple-element.35), channel_id=1, source_target_pairs={{0,2},{1,3},{2,0},{3,1},{4,6},{5,7},{6,4},{7,5},{8,10},{9,11},{10,... | collective-permute-start | bytes 172040 | tf_op jit(solution)/shard_map/ppermute | solution.py:339
  63.4 4.1 %collective-permute-start.20 = (bf16[32,896]{1,0:T(8,128)(2,1)S(1)}, bf16[32,896]{1,0:T(8,128)(2,1)S(1)}, u32[]{:S(2)}, u32[]{:S(2)}) collective-permute-start(bf16[32,896]{1,0:T(8,128)(2,1)S(1)} %get-tuple-element.36), channel_id=1, source_target_pairs={{0,3},{1,2},{2,1},{3,0},{4,7},{5,6},{6,5},{7,4},{8,11},{9,10},{10,... | collective-permute-start | bytes 172040 | tf_op jit(solution)/shard_map/ppermute | solution.py:339
  67.7 5.6 %collective-permute-start.21 = (bf16[8,896]{1,0:T(8,128)(2,1)S(1)}, bf16[8,896]{1,0:T(8,128)(2,1)S(1)}, u32[]{:S(2)}, u32[]{:S(2)}) collective-permute-start(bf16[8,896]{1,0:T(8,128)(2,1)S(1)} %get-tuple-element.40), channel_id=1, source_target_pairs={{0,4},{4,8},{8,12},{12,0},{1,5},{5,9},{9,13},{13,1},{2,6},{6,10},{... | collective-permute-start | bytes 43016 | tf_op jit(solution)/shard_map/ppermute | solution.py:21
  69.7 4.6 %collective-permute-start.22 = (bf16[8,896]{1,0:T(8,128)(2,1)S(1)}, bf16[8,896]{1,0:T(8,128)(2,1)S(1)}, u32[]{:S(2)}, u32[]{:S(2)}) collective-permute-start(bf16[8,896]{1,0:T(8,128)(2,1)S(1)} %get-tuple-element.41), channel_id=1, source_target_pairs={{0,8},{4,12},{8,0},{12,4},{1,9},{5,13},{9,1},{13,5},{2,10},{6,14},... | collective-permute-start | bytes 43016 | tf_op jit(solution)/shard_map/ppermute | solution.py:21
  70.9 3.7 %collective-permute-start.23 = (bf16[8,896]{1,0:T(8,128)(2,1)S(1)}, bf16[8,896]{1,0:T(8,128)(2,1)S(1)}, u32[]{:S(2)}, u32[]{:S(2)}) collective-permute-start(bf16[8,896]{1,0:T(8,128)(2,1)S(1)} %get-tuple-element.42), channel_id=1, source_target_pairs={{0,12},{4,0},{8,4},{12,8},{1,13},{5,1},{9,5},{13,9},{2,14},{6,2},{... | collective-permute-start | bytes 43016 | tf_op jit(solution)/shard_map/ppermute | solution.py:21
  (9 other events, 57.1 us)

commit v3 on v2

--- a/solution.py
+++ b/solution.py
@@ -178,19 +178,24 @@
     return jnp.where(value < 0, value + size, jnp.where(value >= size, value - size, value))
 
 
-def pack_kernel(ctx, groups, query, latent, resid, ids, weights, *outs):
+def pack_kernel(ctx, groups, *refs):
+    query, latent, resid, ids, weights = refs[:5]
+    outs = refs[6:]
     me = lax.axis_index("ctx")
     tok, cols = resid.shape[0], resid.shape[1] // ctx
     rows, width = query.shape
     parts = rows // tok
     lane = lax.broadcasted_iota(jnp.int32, (tok, 128), 1)
-    high = jnp.zeros((tok, 128), F32)
-    for k in range(ids.shape[1]):
-        high = high + jnp.where(lane == ids[:, k : k + 1], weights[:, k : k + 1], 0.0)
-    for k in range(ids.shape[1]):
-        high = high + jnp.where(lane == ids[:, k : k + 1] + 64, weights[:, k : k + 1], 0.0)
-    near = high.astype(BF16).astype(F32)
-    routes = jnp.where(lane < 64, near, high - near)
+    same = lax.broadcasted_iota(jnp.int32, (tok, tok), 0) == lax.broadcasted_iota(
+        jnp.int32, (tok, tok), 1
+    )
+    full = jnp.zeros((tok, 128), F32)
+    for k in range(ids.shape[0]):
+        expert = jnp.sum(jnp.where(same, ids[k : k + 1, :], 0), axis=1, keepdims=True)
+        weight = jnp.sum(jnp.where(same, weights[k : k + 1, :], 0.0), axis=1, keepdims=True)
+        full = full + jnp.where((lane == expert) | (lane == expert + 64), weight, 0.0)
+    near = full.astype(BF16).astype(F32)
+    routes = jnp.where(lane < 64, near, full - near)
     extra = (cols + 128) // parts
     for d, out in enumerate(outs):
         to = wrap(me + d, ctx)
@@ -199,6 +204,28 @@
         out[:, :width] = query[...]
         out[:, width : width + extra] = both.astype(BF16)
         out[:, width + extra :] = latent[...]
+
+
+def open_kernel(out):
+    out[...] = jnp.zeros_like(out)
+
+
+def hold_kernel(value, after, out):
+    out[:16, :128] = value[:16, :128]
+
+
+def hold(value, after):
+    return pl.pallas_call(
+        hold_kernel,
+        out_shape=jax.ShapeDtypeStruct(value.shape, value.dtype),
+        in_specs=[
+            pl.BlockSpec(memory_space=pltpu.VMEM),
+            pl.BlockSpec(memory_space=pl.ANY),
+        ],
+        out_specs=pl.BlockSpec(memory_space=pltpu.VMEM),
+        input_output_aliases={0: 0},
+        compiler_params=pltpu.CompilerParams(vmem_limit_bytes=4 << 20),
+    )(value, after)
 
 
 def attention_kernel(ctx, groups, heads, extra, *refs):
@@ -357,11 +384,18 @@
     like = jax.ShapeDtypeStruct
 
     packed = like((rows, width + extra + latent.shape[1]), BF16)
+    sources = [query, latent, resid, expert_ids.T, route_weights.T]
+    opened = pl.pallas_call(
+        open_kernel,
+        out_shape=like((8, 128), F32),
+        compiler_params=pltpu.CompilerParams(vmem_limit_bytes=1 << 20),
+        cost_estimate=pl.CostEstimate(flops=1 << 31, bytes_accessed=0, transcendentals=0),
+    )()
     packs = call(
         functools.partial(pack_kernel, ctx, groups),
         [packed] * ctx,
-        [query, latent, resid, expert_ids, route_weights],
-        0,
+        sources + [opened],
+        1 << 32,
         8,
     )
     pieces = [packs[0]] + [send(packs[d], "ctx", d) for d in range(1, ctx)]
@@ -399,6 +433,7 @@
         hidden_kernel, like((2 * here, ff), BF16), [mine, sibling, w_gate, w_up], work, 16
     )
     near = around(hidden, ctx)
+    other = hold(other, hidden)
     other_sibling = swap(other, 1)
     hidden = call(
         hidden_kernel, like((2 * here, ff), BF16), [other, other_sibling, w_gate, w_up], work, 16

time: 75.8 us -> 66.8 us (0.88)
  local copies, waits for them, and re-layouts: 9.93 us -> 0.92 us
    unnamed x20 -> x24, local copies, waits for them, and re-layouts: 9.21 us -> 0.91 us
  transfers between devices with their start and end apart: 24 -> 24, of which waited for: 15 -> 16; matrix products, arithmetic and copies ran while one was open for 1% -> 0% of each run, Pallas kernels for 6% -> 6%
where the time goes in v3:
time: 66.8 us; the launch traced here: 66.6 us
  starting transfers between devices  30.3 us (45%)
  waiting for transfers between devices  28.9 us (43%)
  Pallas kernels  6.43 us (10%)
  local copies, waits for them, and re-layouts  0.92 us (1%)
    ppermute x15, starting transfers between devices, send(): lax.ppermute(value, axis, [(i, (i + step) % size) for i in range(size)])  25.5 us
    ppermute x15, waiting for transfers between devices, send(): lax.ppermute(value, axis, [(i, (i + step) % size) for i in range(size)])  15.9 us
    ppermute x9, waiting for transfers between devices, swap(): return lax.ppermute(value, EH, [(i, i ^ step) for i in range(size)])  13 us
    pallas_call x8, Pallas kernels, call(): pl.pallas_call(kernel, out_shape=out, in_specs=[pl.BlockSpec(memory_space...  5.16 us
    ppermute x9, starting transfers between devices, swap(): return lax.ppermute(value, EH, [(i, i ^ step) for i in range(size)])  4.79 us
  transfers between devices with their start and end apart: 24, of which 16 were waited for; matrix products, arithmetic and copies ran while one was open for 0% of the time, Pallas kernels for 6%

profile of v3, /device:TPU:0, one launch (start us, length us, event | category | flops | bytes accessed | tf_op | source)
XLA Modules:
  0.0 66.6 jit_solution(3822312635864184407)
XLA Ops:
  1.0 3.1 %collective-permute-start = (bf16[32,1600]{1,0:T(8,128)(2,1)S(1)}, bf16[32,1600]{1,0:T(8,128)(2,1)S(1)}, u32[]{:S(2)}, u32[]{:S(2)}) collective-permute-start(bf16[32,1600]{1,0:T(8,128)(2,1)S(1)} %get-tuple-element.25), channel_id=1, source_target_pairs={{0,4},{4,8},{8,12},{12,0},{1,5},{5,9},{9,13},{13,1},{2,6},{6,10},{... | collective-permute-start | bytes 307208 | tf_op jit(solution)/shard_map/ppermute | solution.py:21
  4.1 2.6 %collective-permute-start.1 = (bf16[32,1600]{1,0:T(8,128)(2,1)S(1)}, bf16[32,1600]{1,0:T(8,128)(2,1)S(1)}, u32[]{:S(2)}, u32[]{:S(2)}) collective-permute-start(bf16[32,1600]{1,0:T(8,128)(2,1)S(1)} %get-tuple-element.26), channel_id=1, source_target_pairs={{0,8},{4,12},{8,0},{12,4},{1,9},{5,13},{9,1},{13,5},{2,10},{6,14},... | collective-permute-start | bytes 307208 | tf_op jit(solution)/shard_map/ppermute | solution.py:21
  6.7 1.3 %collective-permute-start.2 = (bf16[32,1600]{1,0:T(8,128)(2,1)S(1)}, bf16[32,1600]{1,0:T(8,128)(2,1)S(1)}, u32[]{:S(2)}, u32[]{:S(2)}) collective-permute-start(bf16[32,1600]{1,0:T(8,128)(2,1)S(1)} %get-tuple-element.27), channel_id=1, source_target_pairs={{0,12},{4,0},{8,4},{12,8},{1,13},{5,1},{9,5},{13,9},{2,14},{6,2},{... | collective-permute-start | bytes 307208 | tf_op jit(solution)/shard_map/ppermute | solution.py:21
  8.1 2.0 %collective-permute-done.refs_1_.refs_5_ = bf16[32,1600]{1,0:T(8,128)(2,1)S(1)} collective-permute-done((bf16[32,1600]{1,0:T(8,128)(2,1)S(1)}, bf16[32,1600]{1,0:T(8,128)(2,1)S(1)}, u32[]{:S(2)}, u32[]{:S(2)}) %collective-permute-start) | collective-permute-done | bytes 102432 | tf_op jit(solution)/shard_map/ppermute | solution.py:21
  10.0 3.8 %collective-permute-done.1.refs_2_.refs_6_ = bf16[32,1600]{1,0:T(8,128)(2,1)S(1)} collective-permute-done((bf16[32,1600]{1,0:T(8,128)(2,1)S(1)}, bf16[32,1600]{1,0:T(8,128)(2,1)S(1)}, u32[]{:S(2)}, u32[]{:S(2)}) %collective-permute-start.1) | collective-permute-done | bytes 102432 | tf_op jit(solution)/shard_map/ppermute | solution.py:21
  15.0 1.6 %collective-permute-start.4 = (bf16[32,896]{1,0:T(8,128)(2,1)S(1)}, bf16[32,896]{1,0:T(8,128)(2,1)S(1)}, u32[]{:S(2)}, u32[]{:S(2)}) collective-permute-start(bf16[32,896]{1,0:T(8,128)(2,1)S(1)} %get-tuple-element.30), channel_id=1, source_target_pairs={{0,2},{1,3},{2,0},{3,1},{4,6},{5,7},{6,4},{7,5},{8,10},{9,11},{10,... | collective-permute-start | bytes 172040 | tf_op jit(solution)/shard_map/ppermute | solution.py:366
  16.9 2.5 %collective-permute-done.4.refs_2_ = bf16[32,896]{1,0:T(8,128)(2,1)S(1)} collective-permute-done((bf16[32,896]{1,0:T(8,128)(2,1)S(1)}, bf16[32,896]{1,0:T(8,128)(2,1)S(1)}, u32[]{:S(2)}, u32[]{:S(2)}) %collective-permute-start.4) | collective-permute-done | bytes 57376 | tf_op jit(solution)/shard_map/ppermute | solution.py:366
  20.5 2.8 %collective-permute-start.6 = (bf16[32,896]{1,0:T(8,128)(2,1)S(1)}, bf16[32,896]{1,0:T(8,128)(2,1)S(1)}, u32[]{:S(2)}, u32[]{:S(2)}) collective-permute-start(bf16[32,896]{1,0:T(8,128)(2,1)S(1)} %get-tuple-element.32.refs_0_), channel_id=1, source_target_pairs={{0,4},{4,8},{8,12},{12,0},{1,5},{5,9},{9,13},{13,1},{2,6},{6,10},{... | collective-permute-start | bytes 172040 | tf_op jit(solution)/shard_map/ppermute | solution.py:21
  23.3 1.6 %collective-permute-start.7 = (bf16[32,896]{1,0:T(8,128)(2,1)S(1)}, bf16[32,896]{1,0:T(8,128)(2,1)S(1)}, u32[]{:S(2)}, u32[]{:S(2)}) collective-permute-start(bf16[32,896]{1,0:T(8,128)(2,1)S(1)} %get-tuple-element.32.refs_0_), channel_id=1, source_target_pairs={{0,8},{4,12},{8,0},{12,4},{1,9},{5,13},{9,1},{13,5},{2,10},{6,14},... | collective-permute-start | bytes 172040 | tf_op jit(solution)/shard_map/ppermute | solution.py:21
  26.8 2.4 %collective-permute-done.7.refs_2_ = bf16[32,896]{1,0:T(8,128)(2,1)S(1)} collective-permute-done((bf16[32,896]{1,0:T(8,128)(2,1)S(1)}, bf16[32,896]{1,0:T(8,128)(2,1)S(1)}, u32[]{:S(2)}, u32[]{:S(2)}) %collective-permute-start.7) | collective-permute-done | bytes 57376 | tf_op jit(solution)/shard_map/ppermute | solution.py:21
  29.9 1.3 %collective-permute-start.14 = (bf16[32,3584]{1,0:T(8,128)(2,1)S(1)}, bf16[32,3584]{1,0:T(8,128)(2,1)S(1)}, u32[]{:S(2)}, u32[]{:S(2)}) collective-permute-start(bf16[32,3584]{1,0:T(8,128)(2,1)S(1)} %shard_map.122.near), channel_id=1, source_target_pairs={{0,2},{1,3},{2,0},{3,1},{4,6},{5,7},{6,4},{7,5},{8,10},{9,11},{10,... | collective-permute-start | bytes 688136 | tf_op jit(solution)/shard_map/ppermute | solution.py:366
  31.4 1.4 %shard_map.123.refs_0_.after = bf16[64,512]{1,0:T(8,128)(2,1)S(1)} custom-call(bf16[32,3584]{1,0:T(8,128)(2,1)S(1)} %shard_map.122.near, bf16[32,3584]{1,0:T(8,128)(2,1)S(1)} %collective-permute-done.9.far, bf16[1,3584,512]{2,1,0:T(8,128)(2,1)S(1)} %copy-done, bf16[1,3584,512]{2,1,0:T(8,128)(2,1)S(1)} %copy-done.1), custom_call_target="tpu_custom_call" | custom-call | flops 469762048 | bytes 7798784 | tf_op jit(solution)/shard_map/pallas_call | solution.py:164
  32.8 5.2 %collective-permute-done.14.value = bf16[32,3584]{1,0:T(8,128)(2,1)S(1)} collective-permute-done((bf16[32,3584]{1,0:T(8,128)(2,1)S(1)}, bf16[32,3584]{1,0:T(8,128)(2,1)S(1)}, u32[]{:S(2)}, u32[]{:S(2)}) %collective-permute-start.14) | collective-permute-done | bytes 229408 | tf_op jit(solution)/shard_map/ppermute | solution.py:366
  38.0 1.2 %collective-permute-start.10 = (bf16[64,512]{1,0:T(8,128)(2,1)S(1)}, bf16[64,512]{1,0:T(8,128)(2,1)S(1)}, u32[]{:S(2)}, u32[]{:S(2)}) collective-permute-start(bf16[64,512]{1,0:T(8,128)(2,1)S(1)} %shard_map.123.refs_0_.after), channel_id=1, source_target_pairs={{0,4},{4,8},{8,12},{12,0},{1,5},{5,9},{9,13},{13,1},{2,6},{6,10},{... | collective-permute-start | bytes 196616 | tf_op jit(solution)/shard_map/ppermute | solution.py:21
  39.2 1.7 %collective-permute-start.11 = (bf16[64,512]{1,0:T(8,128)(2,1)S(1)}, bf16[64,512]{1,0:T(8,128)(2,1)S(1)}, u32[]{:S(2)}, u32[]{:S(2)}) collective-permute-start(bf16[64,512]{1,0:T(8,128)(2,1)S(1)} %shard_map.123.refs_0_.after), channel_id=1, source_target_pairs={{0,8},{4,12},{8,0},{12,4},{1,9},{5,13},{9,1},{13,5},{2,10},{6,14},... | collective-permute-start | bytes 196616 | tf_op jit(solution)/shard_map/ppermute | solution.py:21
  41.8 1.4 %shard_map.126.refs_0_ = bf16[64,512]{1,0:T(8,128)(2,1)S(1)} custom-call(bf16[32,3584]{1,0:T(8,128)(2,1)S(1)} %shard_map.125.near, bf16[32,3584]{1,0:T(8,128)(2,1)S(1)} %collective-permute-done.15.far, bf16[1,3584,512]{2,1,0:T(8,128)(2,1)S(1)} %copy-done, bf16[1,3584,512]{2,1,0:T(8,128)(2,1)S(1)} %copy-done.1), custom_call_target="tpu_custom_call" | custom-call | flops 469762048 | bytes 7798784 | tf_op jit(solution)/shard_map/pallas_call | solution.py:164
  44.3 1.2 %collective-permute-start.17 = (bf16[64,512]{1,0:T(8,128)(2,1)S(1)}, bf16[64,512]{1,0:T(8,128)(2,1)S(1)}, u32[]{:S(2)}, u32[]{:S(2)}) collective-permute-start(bf16[64,512]{1,0:T(8,128)(2,1)S(1)} %shard_map.126.refs_0_), channel_id=1, source_target_pairs={{0,8},{4,12},{8,0},{12,4},{1,9},{5,13},{9,1},{13,5},{2,10},{6,14},... | collective-permute-start | bytes 196616 | tf_op jit(solution)/shard_map/ppermute | solution.py:21
  45.6 2.6 %collective-permute-start.18 = (bf16[64,512]{1,0:T(8,128)(2,1)S(1)}, bf16[64,512]{1,0:T(8,128)(2,1)S(1)}, u32[]{:S(2)}, u32[]{:S(2)}) collective-permute-start(bf16[64,512]{1,0:T(8,128)(2,1)S(1)} %shard_map.126.refs_0_), channel_id=1, source_target_pairs={{0,12},{4,0},{8,4},{12,8},{1,13},{5,1},{9,5},{13,9},{2,14},{6,2},{... | collective-permute-start | bytes 196616 | tf_op jit(solution)/shard_map/ppermute | solution.py:21
  50.0 2.7 %collective-permute-done.17.refs_2_ = bf16[64,512]{1,0:T(8,128)(2,1)S(1)} collective-permute-done((bf16[64,512]{1,0:T(8,128)(2,1)S(1)}, bf16[64,512]{1,0:T(8,128)(2,1)S(1)}, u32[]{:S(2)}, u32[]{:S(2)}) %collective-permute-start.17) | collective-permute-done | bytes 65568 | tf_op jit(solution)/shard_map/ppermute | solution.py:21
  53.5 1.4 %collective-permute-start.19 = (bf16[32,896]{1,0:T(8,128)(2,1)S(1)}, bf16[32,896]{1,0:T(8,128)(2,1)S(1)}, u32[]{:S(2)}, u32[]{:S(2)}) collective-permute-start(bf16[32,896]{1,0:T(8,128)(2,1)S(1)} %get-tuple-element.35), channel_id=1, source_target_pairs={{0,2},{1,3},{2,0},{3,1},{4,6},{5,7},{6,4},{7,5},{8,10},{9,11},{10,... | collective-permute-start | bytes 172040 | tf_op jit(solution)/shard_map/ppermute | solution.py:366
  54.9 2.9 %collective-permute-done.19.refs_2_ = bf16[32,896]{1,0:T(8,128)(2,1)S(1)} collective-permute-done((bf16[32,896]{1,0:T(8,128)(2,1)S(1)}, bf16[32,896]{1,0:T(8,128)(2,1)S(1)}, u32[]{:S(2)}, u32[]{:S(2)}) %collective-permute-start.19) | collective-permute-done | bytes 57376 | tf_op jit(solution)/shard_map/ppermute | solution.py:366
  57.8 1.2 %collective-permute-done.20.refs_3_ = bf16[32,896]{1,0:T(8,128)(2,1)S(1)} collective-permute-done((bf16[32,896]{1,0:T(8,128)(2,1)S(1)}, bf16[32,896]{1,0:T(8,128)(2,1)S(1)}, u32[]{:S(2)}, u32[]{:S(2)}) %collective-permute-start.20) | collective-permute-done | bytes 57376 | tf_op jit(solution)/shard_map/ppermute | solution.py:366
  59.1 1.9 %collective-permute-start.21 = (bf16[8,896]{1,0:T(8,128)(2,1)S(1)}, bf16[8,896]{1,0:T(8,128)(2,1)S(1)}, u32[]{:S(2)}, u32[]{:S(2)}) collective-permute-start(bf16[8,896]{1,0:T(8,128)(2,1)S(1)} %get-tuple-element.40), channel_id=1, source_target_pairs={{0,4},{4,8},{8,12},{12,0},{1,5},{5,9},{9,13},{13,1},{2,6},{6,10},{... | collective-permute-start | bytes 43016 | tf_op jit(solution)/shard_map/ppermute | solution.py:21
  63.5 1.2 %collective-permute-done.21.refs_1_ = bf16[8,896]{1,0:T(8,128)(2,1)S(1)} collective-permute-done((bf16[8,896]{1,0:T(8,128)(2,1)S(1)}, bf16[8,896]{1,0:T(8,128)(2,1)S(1)}, u32[]{:S(2)}, u32[]{:S(2)}) %collective-permute-start.21) | collective-permute-done | bytes 14368 | tf_op jit(solution)/shard_map/ppermute | solution.py:21
  (61 shorter events, 15.5 us)
Async XLA Ops:
  1.0 9.0 %collective-permute-start = (bf16[32,1600]{1,0:T(8,128)(2,1)S(1)}, bf16[32,1600]{1,0:T(8,128)(2,1)S(1)}, u32[]{:S(2)}, u32[]{:S(2)}) collective-permute-start(bf16[32,1600]{1,0:T(8,128)(2,1)S(1)} %get-tuple-element.25), channel_id=1, source_target_pairs={{0,4},{4,8},{8,12},{12,0},{1,5},{5,9},{9,13},{13,1},{2,6},{6,10},{... | collective-permute-start | bytes 307208 | tf_op jit(solution)/shard_map/ppermute | solution.py:21
  4.1 9.7 %collective-permute-start.1 = (bf16[32,1600]{1,0:T(8,128)(2,1)S(1)}, bf16[32,1600]{1,0:T(8,128)(2,1)S(1)}, u32[]{:S(2)}, u32[]{:S(2)}) collective-permute-start(bf16[32,1600]{1,0:T(8,128)(2,1)S(1)} %get-tuple-element.26), channel_id=1, source_target_pairs={{0,8},{4,12},{8,0},{12,4},{1,9},{5,13},{9,1},{13,5},{2,10},{6,14},... | collective-permute-start | bytes 307208 | tf_op jit(solution)/shard_map/ppermute | solution.py:21
  6.7 7.1 %collective-permute-start.2 = (bf16[32,1600]{1,0:T(8,128)(2,1)S(1)}, bf16[32,1600]{1,0:T(8,128)(2,1)S(1)}, u32[]{:S(2)}, u32[]{:S(2)}) collective-permute-start(bf16[32,1600]{1,0:T(8,128)(2,1)S(1)} %get-tuple-element.27), channel_id=1, source_target_pairs={{0,12},{4,0},{8,4},{12,8},{1,13},{5,1},{9,5},{13,9},{2,14},{6,2},{... | collective-permute-start | bytes 307208 | tf_op jit(solution)/shard_map/ppermute | solution.py:21
  15.0 1.9 %collective-permute-start.3 = (bf16[32,896]{1,0:T(8,128)(2,1)S(1)}, bf16[32,896]{1,0:T(8,128)(2,1)S(1)}, u32[]{:S(2)}, u32[]{:S(2)}) collective-permute-start(bf16[32,896]{1,0:T(8,128)(2,1)S(1)} %get-tuple-element.29), channel_id=1, source_target_pairs={{0,1},{1,0},{2,3},{3,2},{4,5},{5,4},{6,7},{7,6},{8,9},{9,8},{10,11... | collective-permute-start | bytes 172040 | tf_op jit(solution)/shard_map/ppermute | solution.py:366
  15.0 4.3 %collective-permute-start.4 = (bf16[32,896]{1,0:T(8,128)(2,1)S(1)}, bf16[32,896]{1,0:T(8,128)(2,1)S(1)}, u32[]{:S(2)}, u32[]{:S(2)}) collective-permute-start(bf16[32,896]{1,0:T(8,128)(2,1)S(1)} %get-tuple-element.30), channel_id=1, source_target_pairs={{0,2},{1,3},{2,0},{3,1},{4,6},{5,7},{6,4},{7,5},{8,10},{9,11},{10,... | collective-permute-start | bytes 172040 | tf_op jit(solution)/shard_map/ppermute | solution.py:366
  16.6 3.9 %collective-permute-start.5 = (bf16[32,896]{1,0:T(8,128)(2,1)S(1)}, bf16[32,896]{1,0:T(8,128)(2,1)S(1)}, u32[]{:S(2)}, u32[]{:S(2)}) collective-permute-start(bf16[32,896]{1,0:T(8,128)(2,1)S(1)} %get-tuple-element.31), channel_id=1, source_target_pairs={{0,3},{1,2},{2,1},{3,0},{4,7},{5,6},{6,5},{7,4},{8,11},{9,10},{10,... | collective-permute-start | bytes 172040 | tf_op jit(solution)/shard_map/ppermute | solution.py:366
  20.5 6.2 %collective-permute-start.6 = (bf16[32,896]{1,0:T(8,128)(2,1)S(1)}, bf16[32,896]{1,0:T(8,128)(2,1)S(1)}, u32[]{:S(2)}, u32[]{:S(2)}) collective-permute-start(bf16[32,896]{1,0:T(8,128)(2,1)S(1)} %get-tuple-element.32.refs_0_), channel_id=1, source_target_pairs={{0,4},{4,8},{8,12},{12,0},{1,5},{5,9},{9,13},{13,1},{2,6},{6,10},{... | collective-permute-start | bytes 172040 | tf_op jit(solution)/shard_map/ppermute | solution.py:21
  23.3 5.8 %collective-permute-start.7 = (bf16[32,896]{1,0:T(8,128)(2,1)S(1)}, bf16[32,896]{1,0:T(8,128)(2,1)S(1)}, u32[]{:S(2)}, u32[]{:S(2)}) collective-permute-start(bf16[32,896]{1,0:T(8,128)(2,1)S(1)} %get-tuple-element.32.refs_0_), channel_id=1, source_target_pairs={{0,8},{4,12},{8,0},{12,4},{1,9},{5,13},{9,1},{13,5},{2,10},{6,14},... | collective-permute-start | bytes 172040 | tf_op jit(solution)/shard_map/ppermute | solution.py:21
  24.9 4.8 %collective-permute-start.8 = (bf16[32,896]{1,0:T(8,128)(2,1)S(1)}, bf16[32,896]{1,0:T(8,128)(2,1)S(1)}, u32[]{:S(2)}, u32[]{:S(2)}) collective-permute-start(bf16[32,896]{1,0:T(8,128)(2,1)S(1)} %get-tuple-element.32.refs_0_), channel_id=1, source_target_pairs={{0,12},{4,0},{8,4},{12,8},{1,13},{5,1},{9,5},{13,9},{2,14},{6,2},{... | collective-permute-start | bytes 172040 | tf_op jit(solution)/shard_map/ppermute | solution.py:21
  29.9 1.6 %collective-permute-start.9 = (bf16[32,3584]{1,0:T(8,128)(2,1)S(1)}, bf16[32,3584]{1,0:T(8,128)(2,1)S(1)}, u32[]{:S(2)}, u32[]{:S(2)}) collective-permute-start(bf16[32,3584]{1,0:T(8,128)(2,1)S(1)} %shard_map.122.near), channel_id=1, source_target_pairs={{0,1},{1,0},{2,3},{3,2},{4,5},{5,4},{6,7},{7,6},{8,9},{9,8},{10,11... | collective-permute-start | bytes 688136 | tf_op jit(solution)/shard_map/ppermute | solution.py:366
  29.9 8.0 %collective-permute-start.14 = (bf16[32,3584]{1,0:T(8,128)(2,1)S(1)}, bf16[32,3584]{1,0:T(8,128)(2,1)S(1)}, u32[]{:S(2)}, u32[]{:S(2)}) collective-permute-start(bf16[32,3584]{1,0:T(8,128)(2,1)S(1)} %shard_map.122.near), channel_id=1, source_target_pairs={{0,2},{1,3},{2,0},{3,1},{4,6},{5,7},{6,4},{7,5},{8,10},{9,11},{10,... | collective-permute-start | bytes 688136 | tf_op jit(solution)/shard_map/ppermute | solution.py:366
  38.0 3.9 %collective-permute-start.15 = (bf16[32,3584]{1,0:T(8,128)(2,1)S(1)}, bf16[32,3584]{1,0:T(8,128)(2,1)S(1)}, u32[]{:S(2)}, u32[]{:S(2)}) collective-permute-start(bf16[32,3584]{1,0:T(8,128)(2,1)S(1)} %shard_map.125.near), channel_id=1, source_target_pairs={{0,1},{1,0},{2,3},{3,2},{4,5},{5,4},{6,7},{7,6},{8,9},{9,8},{10,11... | collective-permute-start | bytes 688136 | tf_op jit(solution)/shard_map/ppermute | solution.py:366
  38.0 7.6 %collective-permute-start.10 = (bf16[64,512]{1,0:T(8,128)(2,1)S(1)}, bf16[64,512]{1,0:T(8,128)(2,1)S(1)}, u32[]{:S(2)}, u32[]{:S(2)}) collective-permute-start(bf16[64,512]{1,0:T(8,128)(2,1)S(1)} %shard_map.123.refs_0_.after), channel_id=1, source_target_pairs={{0,4},{4,8},{8,12},{12,0},{1,5},{5,9},{9,13},{13,1},{2,6},{6,10},{... | collective-permute-start | bytes 196616 | tf_op jit(solution)/shard_map/ppermute | solution.py:21
  39.2 9.0 %collective-permute-start.11 = (bf16[64,512]{1,0:T(8,128)(2,1)S(1)}, bf16[64,512]{1,0:T(8,128)(2,1)S(1)}, u32[]{:S(2)}, u32[]{:S(2)}) collective-permute-start(bf16[64,512]{1,0:T(8,128)(2,1)S(1)} %shard_map.123.refs_0_.after), channel_id=1, source_target_pairs={{0,8},{4,12},{8,0},{12,4},{1,9},{5,13},{9,1},{13,5},{2,10},{6,14},... | collective-permute-start | bytes 196616 | tf_op jit(solution)/shard_map/ppermute | solution.py:21
  40.9 7.4 %collective-permute-start.12 = (bf16[64,512]{1,0:T(8,128)(2,1)S(1)}, bf16[64,512]{1,0:T(8,128)(2,1)S(1)}, u32[]{:S(2)}, u32[]{:S(2)}) collective-permute-start(bf16[64,512]{1,0:T(8,128)(2,1)S(1)} %shard_map.123.refs_0_.after), channel_id=1, source_target_pairs={{0,12},{4,0},{8,4},{12,8},{1,13},{5,1},{9,5},{13,9},{2,14},{6,2},{... | collective-permute-start | bytes 196616 | tf_op jit(solution)/shard_map/ppermute | solution.py:21
  43.2 6.8 %collective-permute-start.16 = (bf16[64,512]{1,0:T(8,128)(2,1)S(1)}, bf16[64,512]{1,0:T(8,128)(2,1)S(1)}, u32[]{:S(2)}, u32[]{:S(2)}) collective-permute-start(bf16[64,512]{1,0:T(8,128)(2,1)S(1)} %shard_map.126.refs_0_), channel_id=1, source_target_pairs={{0,4},{4,8},{8,12},{12,0},{1,5},{5,9},{9,13},{13,1},{2,6},{6,10},{... | collective-permute-start | bytes 196616 | tf_op jit(solution)/shard_map/ppermute | solution.py:21
  44.3 8.5 %collective-permute-start.17 = (bf16[64,512]{1,0:T(8,128)(2,1)S(1)}, bf16[64,512]{1,0:T(8,128)(2,1)S(1)}, u32[]{:S(2)}, u32[]{:S(2)}) collective-permute-start(bf16[64,512]{1,0:T(8,128)(2,1)S(1)} %shard_map.126.refs_0_), channel_id=1, source_target_pairs={{0,8},{4,12},{8,0},{12,4},{1,9},{5,13},{9,1},{13,5},{2,10},{6,14},... | collective-permute-start | bytes 196616 | tf_op jit(solution)/shard_map/ppermute | solution.py:21
  45.6 7.2 %collective-permute-start.18 = (bf16[64,512]{1,0:T(8,128)(2,1)S(1)}, bf16[64,512]{1,0:T(8,128)(2,1)S(1)}, u32[]{:S(2)}, u32[]{:S(2)}) collective-permute-start(bf16[64,512]{1,0:T(8,128)(2,1)S(1)} %shard_map.126.refs_0_), channel_id=1, source_target_pairs={{0,12},{4,0},{8,4},{12,8},{1,13},{5,1},{9,5},{13,9},{2,14},{6,2},{... | collective-permute-start | bytes 196616 | tf_op jit(solution)/shard_map/ppermute | solution.py:21
  49.0 5.9 %collective-permute-start.13 = (bf16[32,896]{1,0:T(8,128)(2,1)S(1)}, bf16[32,896]{1,0:T(8,128)(2,1)S(1)}, u32[]{:S(2)}, u32[]{:S(2)}) collective-permute-start(bf16[32,896]{1,0:T(8,128)(2,1)S(1)} %get-tuple-element.34), channel_id=1, source_target_pairs={{0,1},{1,0},{2,3},{3,2},{4,5},{5,4},{6,7},{7,6},{8,9},{9,8},{10,11... | collective-permute-start | bytes 172040 | tf_op jit(solution)/shard_map/ppermute | solution.py:366
  53.5 4.2 %collective-permute-start.19 = (bf16[32,896]{1,0:T(8,128)(2,1)S(1)}, bf16[32,896]{1,0:T(8,128)(2,1)S(1)}, u32[]{:S(2)}, u32[]{:S(2)}) collective-permute-start(bf16[32,896]{1,0:T(8,128)(2,1)S(1)} %get-tuple-element.35), channel_id=1, source_target_pairs={{0,2},{1,3},{2,0},{3,1},{4,6},{5,7},{6,4},{7,5},{8,10},{9,11},{10,... | collective-permute-start | bytes 172040 | tf_op jit(solution)/shard_map/ppermute | solution.py:366
  54.9 4.1 %collective-permute-start.20 = (bf16[32,896]{1,0:T(8,128)(2,1)S(1)}, bf16[32,896]{1,0:T(8,128)(2,1)S(1)}, u32[]{:S(2)}, u32[]{:S(2)}) collective-permute-start(bf16[32,896]{1,0:T(8,128)(2,1)S(1)} %get-tuple-element.36), channel_id=1, source_target_pairs={{0,3},{1,2},{2,1},{3,0},{4,7},{5,6},{6,5},{7,4},{8,11},{9,10},{10,... | collective-permute-start | bytes 172040 | tf_op jit(solution)/shard_map/ppermute | solution.py:366
  59.1 5.6 %collective-permute-start.21 = (bf16[8,896]{1,0:T(8,128)(2,1)S(1)}, bf16[8,896]{1,0:T(8,128)(2,1)S(1)}, u32[]{:S(2)}, u32[]{:S(2)}) collective-permute-start(bf16[8,896]{1,0:T(8,128)(2,1)S(1)} %get-tuple-element.40), channel_id=1, source_target_pairs={{0,4},{4,8},{8,12},{12,0},{1,5},{5,9},{9,13},{13,1},{2,6},{6,10},{... | collective-permute-start | bytes 43016 | tf_op jit(solution)/shard_map/ppermute | solution.py:21
  61.1 4.6 %collective-permute-start.22 = (bf16[8,896]{1,0:T(8,128)(2,1)S(1)}, bf16[8,896]{1,0:T(8,128)(2,1)S(1)}, u32[]{:S(2)}, u32[]{:S(2)}) collective-permute-start(bf16[8,896]{1,0:T(8,128)(2,1)S(1)} %get-tuple-element.41), channel_id=1, source_target_pairs={{0,8},{4,12},{8,0},{12,4},{1,9},{5,13},{9,1},{13,5},{2,10},{6,14},... | collective-permute-start | bytes 43016 | tf_op jit(solution)/shard_map/ppermute | solution.py:21
  62.3 3.7 %collective-permute-start.23 = (bf16[8,896]{1,0:T(8,128)(2,1)S(1)}, bf16[8,896]{1,0:T(8,128)(2,1)S(1)}, u32[]{:S(2)}, u32[]{:S(2)}) collective-permute-start(bf16[8,896]{1,0:T(8,128)(2,1)S(1)} %get-tuple-element.42), channel_id=1, source_target_pairs={{0,12},{4,0},{8,4},{12,8},{1,13},{5,1},{9,5},{13,9},{2,14},{6,2},{... | collective-permute-start | bytes 43016 | tf_op jit(solution)/shard_map/ppermute | solution.py:21
  (12 other events, 138.8 us)

commit v4 on v3

--- a/solution.py
+++ b/solution.py
@@ -210,22 +210,20 @@
     out[...] = jnp.zeros_like(out)
 
 
-def hold_kernel(value, after, out):
+def hold_kernel(value, *rest):
+    out = rest[-1]
     out[:16, :128] = value[:16, :128]
 
 
-def hold(value, after):
+def hold(value, *after):
     return pl.pallas_call(
         hold_kernel,
         out_shape=jax.ShapeDtypeStruct(value.shape, value.dtype),
-        in_specs=[
-            pl.BlockSpec(memory_space=pltpu.VMEM),
-            pl.BlockSpec(memory_space=pl.ANY),
-        ],
+        in_specs=[pl.BlockSpec(memory_space=pltpu.VMEM)] * (1 + len(after)),
         out_specs=pl.BlockSpec(memory_space=pltpu.VMEM),
         input_output_aliases={0: 0},
         compiler_params=pltpu.CompilerParams(vmem_limit_bytes=4 << 20),
-    )(value, after)
+    )(value, *after)
 
 
 def attention_kernel(ctx, groups, heads, extra, *refs):
@@ -300,56 +298,69 @@
 
 
 def norm_kernel(ctx, *refs):
-    columns, gain, out = refs[:ctx], refs[ctx], refs[ctx + 1]
+    columns, gain, routes, out = refs[:ctx], refs[ctx], refs[ctx + 1], refs[ctx + 2]
     me = lax.axis_index("ctx")
     cols = columns[0].shape[1]
+    model = ctx * cols
     values = [c[...].astype(F32) for c in columns]
     squares = values[0] * values[0]
     for v in values[1:]:
         squares = squares + v * v
-    mean = jnp.sum(squares, axis=1, keepdims=True) * (1.0 / out.shape[1])
+    mean = jnp.sum(squares, axis=1, keepdims=True) * (1.0 / model)
     inverse = lax.rsqrt(mean + 1e-06)
     for d, v in enumerate(values):
         at = pl.ds(pl.multiple_of(wrap(me - d, ctx) * cols, 128), cols)
         out[:, at] = (v * inverse * gain[:, at]).astype(BF16)
+    out[:, model:] = jnp.concatenate([routes[b] for b in range(ctx)], axis=0).astype(BF16)
 
 
 def hidden_kernel(near, far, w_gate, w_up, out):
-    rows = jnp.concatenate([near[...], far[...]], axis=0)
+    model = w_gate.shape[1]
+    rows = jnp.concatenate([near[:, :model], far[:, :model]], axis=0)
     gate_part = jnp.dot(rows, w_gate[0], preferred_element_type=F32)
     up_part = jnp.dot(rows, w_up[0], preferred_element_type=F32)
     out[...] = (gate_part / (1.0 + jnp.exp(-gate_part)) * up_part).astype(BF16)
 
 
-def down_kernel(ctx, *refs):
-    hidden, w_down, outs = refs[:ctx], refs[ctx], refs[ctx + 1 :]
+def down(ctx, hidden, w_down):
     me = lax.axis_index("ctx")
     ff = hidden[0].shape[1]
     total = 0.0
     for d in range(ctx):
         at = pl.ds(pl.multiple_of(wrap(me - d, ctx) * ff, ff), ff)
         total = total + jnp.dot(hidden[d][...], w_down[0, at, :], preferred_element_type=F32)
-    rows = outs[0].shape[0]
-    for n, out in enumerate(outs):
-        out[...] = total[n * rows : (n + 1) * rows].astype(BF16)
-
-
-def combine_kernel(ctx, groups, *refs):
-    parts, kept, routes, outs = refs[:groups], refs[groups], refs[groups + 1], refs[groups + 2 : -1]
-    final = refs[-1]
-    me, mine = lax.axis_index("ctx"), lax.axis_index(EH)
-    tok, cols = kept.shape[1:]
-    weights = jnp.concatenate([routes[b] for b in range(ctx)], axis=0)
-    total = jnp.concatenate([kept[b] for b in range(ctx)], axis=0)
-    lane = lax.broadcasted_iota(jnp.int32, weights.shape, 1)
-    for s, part in enumerate(parts):
-        expert = jnp.bitwise_xor(mine, s)
-        here = (lane == expert) | (lane == expert + 64)
-        weight = jnp.sum(jnp.where(here, weights, 0.0), axis=1, keepdims=True)
-        total = total + part[...].astype(F32) * weight
+    return total
+
+
+def weight_of(routes, expert):
+    lane = lax.broadcasted_iota(jnp.int32, routes.shape, 1)
+    here = (lane == expert) | (lane == expert + 64)
+    return jnp.sum(jnp.where(here, routes, 0.0), axis=1, keepdims=True)
+
+
+def product_kernel(ctx, *refs):
+    hidden, w_down, own_in, other_in, base = refs[:ctx], *refs[ctx : ctx + 4]
+    own, other = refs[-2:]
+    total = down(ctx, hidden, w_down)
+    rows, model = own.shape[0], own_in.shape[1] - 128
+    mine = lax.axis_index(EH)
+    own_weight = weight_of(own_in[:, model:].astype(F32), mine)
+    own_total = total[:rows] * own_weight
+    if base.ndim == 3:
+        own_total = own_total + jnp.concatenate([base[b] for b in range(ctx)], axis=0)
+    own[...] = own_total
+    other_weight = weight_of(other_in[:, model:].astype(F32), mine)
+    other[...] = (total[rows:] * other_weight).astype(other.dtype)
+
+
+def finish_kernel(ctx, own, given, started, joined, *outs):
+    final = outs[-1]
+    me = lax.axis_index("ctx")
+    tok = outs[0].shape[0]
+    total = started[...] + joined[...].astype(F32) + own[...] + given[...].astype(F32)
     for b in range(ctx):
         final[b] = total[b * tok : (b + 1) * tok]
-    for d, out in enumerate(outs):
+    for d, out in enumerate(outs[:-1]):
         out[...] = final[wrap(me + d, ctx)].astype(BF16)
 
 
@@ -359,6 +370,16 @@
     cols = parts[0].shape[1]
     for d, part in enumerate(parts):
         out[:, pl.ds(pl.multiple_of(wrap(me - d, ctx) * cols, 128), cols)] = part[...]
+
+
+def across(value, step):
+    ctx, exp = lax.axis_size("ctx"), lax.axis_size("exp")
+    pairs = [
+        (c * exp + e, (c + step) % ctx * exp + (e + exp // 2) % exp)
+        for c in range(ctx)
+        for e in range(exp)
+    ]
+    return lax.ppermute(value, ("ctx", "exp"), pairs)
 
 
 def swap(value, step):
@@ -422,8 +443,8 @@
     )
     mine = call(
         functools.partial(norm_kernel, ctx),
-        like((here, model), BF16),
-        around(travelling, ctx) + [norm_gain.reshape(1, model)],
+        like((here, model + 128), BF16),
+        around(travelling, ctx) + [norm_gain.reshape(1, model), routes],
         0,
         8,
     )
@@ -433,29 +454,29 @@
         hidden_kernel, like((2 * here, ff), BF16), [mine, sibling, w_gate, w_up], work, 16
     )
     near = around(hidden, ctx)
-    other = hold(other, hidden)
+    other = hold(other, near[1])
     other_sibling = swap(other, 1)
     hidden = call(
         hidden_kernel, like((2 * here, ff), BF16), [other, other_sibling, w_gate, w_up], work, 16
     )
     far = around(hidden, ctx)
-    down = functools.partial(down_kernel, ctx)
-    pair = [like((here, cols), BF16)] * 2
-    near = call(down, pair, near + [w_down], work // 2, 16)
-    far = call(down, pair, far + [w_down], work // 2, 16)
-    parts = [near[0], swap(near[1], 1), swap(far[0], groups // 2), swap(far[1], groups // 2 + 1)]
+    pair = [like((here, cols), F32), like((here, cols), BF16)]
+    product = functools.partial(product_kernel, ctx)
+    near = call(product, pair, near + [w_down, mine, sibling, kept], work // 2, 16)
+    started, joined = swap(near[0], groups // 2), swap(near[1], groups // 2 + 1)
+    far = call(product, pair, far + [w_down, other, other_sibling, near[1]], work // 2, 16)
     finals = pl.pallas_call(
-        functools.partial(combine_kernel, ctx, groups),
+        functools.partial(finish_kernel, ctx),
         out_shape=[like((tok, cols), BF16)] * ctx,
-        in_specs=[pl.BlockSpec(memory_space=pltpu.VMEM)] * (groups + 2),
+        in_specs=[pl.BlockSpec(memory_space=pltpu.VMEM)] * 4,
         out_specs=[pl.BlockSpec(memory_space=pltpu.VMEM)] * ctx,
         scratch_shapes=[pltpu.VMEM((ctx, tok, cols), F32)],
         compiler_params=pltpu.CompilerParams(vmem_limit_bytes=8 << 20),
-    )(*parts, kept, routes)
+    )(far[0], swap(far[1], 1), started, joined)
     return call(
         functools.partial(gather_kernel, ctx),
         like((tok, model), BF16),
-        [finals[0]] + [send(finals[d], "ctx", d) for d in range(1, ctx)],
+        [across(finals[d], d) for d in range(ctx)],
         0,
         8,
     )
@@ -478,12 +499,14 @@
     )
     experts = mesh.shape["exp"] * mesh.shape["head"]
 
+    chips = mesh.shape["exp"] == 2 and mesh.shape["head"] == 2
+
     def step(*args):
         cols, rows = args[4].shape[1], args[1].shape[0]
         parts = rows // args[5].shape[0]
         whole = cols % 128 == 0 and (cols + 128) % (128 * parts) == 0 and parts == experts
         small = rows * mesh.shape["ctx"] <= 256
-        return (fast_shards if experts == 4 and whole and small else shards)(*args)
+        return (fast_shards if chips and whole and small else shards)(*args)
 
     return jax.shard_map(
         step,

time: 66.8 us -> 64.2 us (0.961)
  waiting for transfers between devices: 28.9 us -> 24.8 us
  starting transfers between devices: 30.3 us -> 31.8 us
    ppermute x0 -> x4, starting transfers between devices: none -> 6.82 us  [across(): return lax.ppermute(value, ('ctx', 'exp'), pairs)]
    ppermute x15 -> x12, starting transfers between devices: 25.5 us -> 20.2 us  [send(): lax.ppermute(value, axis, [(i, (i + step) % size) for i in range(size)])]
    ppermute x9, waiting for transfers between devices: 13 us -> 9.04 us  [swap(): return lax.ppermute(value, EH, [(i, i ^ step) for i in range(size)])]
    ppermute x15 -> x12, waiting for transfers between devices: 15.9 us -> 13.2 us  [send(): lax.ppermute(value, axis, [(i, (i + step) % size) for i in range(size)])]
    ppermute x0 -> x4, waiting for transfers between devices: none -> 2.64 us  [across(): return lax.ppermute(value, ('ctx', 'exp'), pairs)]
  transfers between devices with their start and end apart: 24 -> 25, of which waited for: 16 -> 17; matrix products, arithmetic and copies ran while one was open for 0% -> 0% of each run, Pallas kernels for 6% -> 7%
where the time goes in v4:
time: 64.2 us; the launch traced here: 64.1 us
  starting transfers between devices  31.8 us (50%)
  waiting for transfers between devices  24.8 us (39%)
  Pallas kernels  6.33 us (10%)
  local copies, waits for them, and re-layouts  0.92 us (1%)
    ppermute x12, starting transfers between devices, send(): lax.ppermute(value, axis, [(i, (i + step) % size) for i in range(size)])  20.2 us
    ppermute x12, waiting for transfers between devices, send(): lax.ppermute(value, axis, [(i, (i + step) % size) for i in range(size)])  13.2 us
    ppermute x9, waiting for transfers between devices, swap(): return lax.ppermute(value, EH, [(i, i ^ step) for i in range(size)])  9.04 us
    ppermute x4, starting transfers between devices, across(): return lax.ppermute(value, ('ctx', 'exp'), pairs)  6.82 us
    pallas_call x8, Pallas kernels, call(): pl.pallas_call(kernel, out_shape=out, in_specs=[pl.BlockSpec(memory_space...  5.16 us
    ppermute x9, starting transfers between devices, swap(): return lax.ppermute(value, EH, [(i, i ^ step) for i in range(size)])  4.77 us
    ppermute x4, waiting for transfers between devices, across(): return lax.ppermute(value, ('ctx', 'exp'), pairs)  2.64 us
  transfers between devices with their start and end apart: 25, of which 17 were waited for; matrix products, arithmetic and copies ran while one was open for 0% of the time, Pallas kernels for 7%

profile of v4, /device:TPU:0, one launch (start us, length us, event | category | flops | bytes accessed | tf_op | source)
XLA Modules:
  0.0 64.1 jit_solution(1976075519332637654)
XLA Ops:
  1.0 3.1 %collective-permute-start = (bf16[32,1600]{1,0:T(8,128)(2,1)S(1)}, bf16[32,1600]{1,0:T(8,128)(2,1)S(1)}, u32[]{:S(2)}, u32[]{:S(2)}) collective-permute-start(bf16[32,1600]{1,0:T(8,128)(2,1)S(1)} %get-tuple-element.25), channel_id=1, source_target_pairs={{0,4},{4,8},{8,12},{12,0},{1,5},{5,9},{9,13},{13,1},{2,6},{6,10},{... | collective-permute-start | bytes 307208 | tf_op jit(solution)/shard_map/ppermute | solution.py:21
  4.1 2.6 %collective-permute-start.1 = (bf16[32,1600]{1,0:T(8,128)(2,1)S(1)}, bf16[32,1600]{1,0:T(8,128)(2,1)S(1)}, u32[]{:S(2)}, u32[]{:S(2)}) collective-permute-start(bf16[32,1600]{1,0:T(8,128)(2,1)S(1)} %get-tuple-element.26), channel_id=1, source_target_pairs={{0,8},{4,12},{8,0},{12,4},{1,9},{5,13},{9,1},{13,5},{2,10},{6,14},... | collective-permute-start | bytes 307208 | tf_op jit(solution)/shard_map/ppermute | solution.py:21
  6.7 1.3 %collective-permute-start.2 = (bf16[32,1600]{1,0:T(8,128)(2,1)S(1)}, bf16[32,1600]{1,0:T(8,128)(2,1)S(1)}, u32[]{:S(2)}, u32[]{:S(2)}) collective-permute-start(bf16[32,1600]{1,0:T(8,128)(2,1)S(1)} %get-tuple-element.27), channel_id=1, source_target_pairs={{0,12},{4,0},{8,4},{12,8},{1,13},{5,1},{9,5},{13,9},{2,14},{6,2},{... | collective-permute-start | bytes 307208 | tf_op jit(solution)/shard_map/ppermute | solution.py:21
  8.1 2.0 %collective-permute-done.refs_1_.refs_5_ = bf16[32,1600]{1,0:T(8,128)(2,1)S(1)} collective-permute-done((bf16[32,1600]{1,0:T(8,128)(2,1)S(1)}, bf16[32,1600]{1,0:T(8,128)(2,1)S(1)}, u32[]{:S(2)}, u32[]{:S(2)}) %collective-permute-start) | collective-permute-done | bytes 102432 | tf_op jit(solution)/shard_map/ppermute | solution.py:21
  10.0 3.8 %collective-permute-done.1.refs_2_.refs_6_ = bf16[32,1600]{1,0:T(8,128)(2,1)S(1)} collective-permute-done((bf16[32,1600]{1,0:T(8,128)(2,1)S(1)}, bf16[32,1600]{1,0:T(8,128)(2,1)S(1)}, u32[]{:S(2)}, u32[]{:S(2)}) %collective-permute-start.1) | collective-permute-done | bytes 102432 | tf_op jit(solution)/shard_map/ppermute | solution.py:21
  15.0 1.6 %collective-permute-start.4 = (bf16[32,896]{1,0:T(8,128)(2,1)S(1)}, bf16[32,896]{1,0:T(8,128)(2,1)S(1)}, u32[]{:S(2)}, u32[]{:S(2)}) collective-permute-start(bf16[32,896]{1,0:T(8,128)(2,1)S(1)} %get-tuple-element.30), channel_id=1, source_target_pairs={{0,2},{1,3},{2,0},{3,1},{4,6},{5,7},{6,4},{7,5},{8,10},{9,11},{10,... | collective-permute-start | bytes 172040 | tf_op jit(solution)/shard_map/ppermute | solution.py:387
  16.9 2.5 %collective-permute-done.4.refs_2_ = bf16[32,896]{1,0:T(8,128)(2,1)S(1)} collective-permute-done((bf16[32,896]{1,0:T(8,128)(2,1)S(1)}, bf16[32,896]{1,0:T(8,128)(2,1)S(1)}, u32[]{:S(2)}, u32[]{:S(2)}) %collective-permute-start.4) | collective-permute-done | bytes 57376 | tf_op jit(solution)/shard_map/ppermute | solution.py:387
  20.5 2.8 %collective-permute-start.6 = (bf16[32,896]{1,0:T(8,128)(2,1)S(1)}, bf16[32,896]{1,0:T(8,128)(2,1)S(1)}, u32[]{:S(2)}, u32[]{:S(2)}) collective-permute-start(bf16[32,896]{1,0:T(8,128)(2,1)S(1)} %get-tuple-element.32.refs_0_), channel_id=1, source_target_pairs={{0,4},{4,8},{8,12},{12,0},{1,5},{5,9},{9,13},{13,1},{2,6},{6,10},{... | collective-permute-start | bytes 172040 | tf_op jit(solution)/shard_map/ppermute | solution.py:21
  23.3 1.6 %collective-permute-start.7 = (bf16[32,896]{1,0:T(8,128)(2,1)S(1)}, bf16[32,896]{1,0:T(8,128)(2,1)S(1)}, u32[]{:S(2)}, u32[]{:S(2)}) collective-permute-start(bf16[32,896]{1,0:T(8,128)(2,1)S(1)} %get-tuple-element.32.refs_0_), channel_id=1, source_target_pairs={{0,8},{4,12},{8,0},{12,4},{1,9},{5,13},{9,1},{13,5},{2,10},{6,14},... | collective-permute-start | bytes 172040 | tf_op jit(solution)/shard_map/ppermute | solution.py:21
  26.8 2.4 %collective-permute-done.7.refs_2_ = bf16[32,896]{1,0:T(8,128)(2,1)S(1)} collective-permute-done((bf16[32,896]{1,0:T(8,128)(2,1)S(1)}, bf16[32,896]{1,0:T(8,128)(2,1)S(1)}, u32[]{:S(2)}, u32[]{:S(2)}) %collective-permute-start.7) | collective-permute-done | bytes 57376 | tf_op jit(solution)/shard_map/ppermute | solution.py:21
  29.9 1.3 %collective-permute-start.9 = (bf16[32,3712]{1,0:T(8,128)(2,1)S(1)}, bf16[32,3712]{1,0:T(8,128)(2,1)S(1)}, u32[]{:S(2)}, u32[]{:S(2)}) collective-permute-start(bf16[32,3712]{1,0:T(8,128)(2,1)S(1)} %shard_map.122.near.refs_5_), channel_id=1, source_target_pairs={{0,2},{1,3},{2,0},{3,1},{4,6},{5,7},{6,4},{7,5},{8,10},{9,11},{10,... | collective-permute-start | bytes 712712 | tf_op jit(solution)/shard_map/ppermute | solution.py:387
  31.4 1.4 %shard_map.123.refs_0_ = bf16[64,512]{1,0:T(8,128)(2,1)S(1)} custom-call(bf16[32,3712]{1,0:T(8,128)(2,1)S(1)} %shard_map.122.near.refs_5_, bf16[32,3712]{1,0:T(8,128)(2,1)S(1)} %collective-permute-done.10.far.refs_6_, bf16[1,3584,512]{2,1,0:T(8,128)(2,1)S(1)} %copy-done, bf16[1,3584,512]{2,1,0:T(8,128)(2,1)S(1)} %copy-done.1), custom_call_target="tpu_custom_call" | custom-call | flops 469762048 | bytes 7815168 | tf_op jit(solution)/shard_map/pallas_call | solution.py:164
  32.8 1.2 %collective-permute-start.11 = (bf16[64,512]{1,0:T(8,128)(2,1)S(1)}, bf16[64,512]{1,0:T(8,128)(2,1)S(1)}, u32[]{:S(2)}, u32[]{:S(2)}) collective-permute-start(bf16[64,512]{1,0:T(8,128)(2,1)S(1)} %shard_map.123.refs_0_), channel_id=1, source_target_pairs={{0,4},{4,8},{8,12},{12,0},{1,5},{5,9},{9,13},{13,1},{2,6},{6,10},{... | collective-permute-start | bytes 196616 | tf_op jit(solution)/shard_map/ppermute | solution.py:21
  34.0 4.1 %collective-permute-done.9.value = bf16[32,3712]{1,0:T(8,128)(2,1)S(1)} collective-permute-done((bf16[32,3712]{1,0:T(8,128)(2,1)S(1)}, bf16[32,3712]{1,0:T(8,128)(2,1)S(1)}, u32[]{:S(2)}, u32[]{:S(2)}) %collective-permute-start.9) | collective-permute-done | bytes 237600 | tf_op jit(solution)/shard_map/ppermute | solution.py:387
  39.0 2.8 %collective-permute-start.17 = (bf16[64,512]{1,0:T(8,128)(2,1)S(1)}, bf16[64,512]{1,0:T(8,128)(2,1)S(1)}, u32[]{:S(2)}, u32[]{:S(2)}) collective-permute-start(bf16[64,512]{1,0:T(8,128)(2,1)S(1)} %shard_map.123.refs_0_), channel_id=1, source_target_pairs={{0,12},{4,0},{8,4},{12,8},{1,13},{5,1},{9,5},{13,9},{2,14},{6,2},{... | collective-permute-start | bytes 196616 | tf_op jit(solution)/shard_map/ppermute | solution.py:21
  41.8 1.4 %shard_map.125.refs_0_ = bf16[64,512]{1,0:T(8,128)(2,1)S(1)} custom-call(bf16[32,3712]{1,0:T(8,128)(2,1)S(1)} %shard_map.124.near.refs_5_, bf16[32,3712]{1,0:T(8,128)(2,1)S(1)} %collective-permute-done.12.far.refs_6_, bf16[1,3584,512]{2,1,0:T(8,128)(2,1)S(1)} %copy-done, bf16[1,3584,512]{2,1,0:T(8,128)(2,1)S(1)} %copy-done.1), custom_call_target="tpu_custom_call" | custom-call | flops 469762048 | bytes 7815168 | tf_op jit(solution)/shard_map/pallas_call | solution.py:164
  43.3 2.1 %collective-permute-start.14 = (bf16[64,512]{1,0:T(8,128)(2,1)S(1)}, bf16[64,512]{1,0:T(8,128)(2,1)S(1)}, u32[]{:S(2)}, u32[]{:S(2)}) collective-permute-start(bf16[64,512]{1,0:T(8,128)(2,1)S(1)} %shard_map.125.refs_0_), channel_id=1, source_target_pairs={{0,8},{4,12},{8,0},{12,4},{1,9},{5,13},{9,1},{13,5},{2,10},{6,14},... | collective-permute-start | bytes 196616 | tf_op jit(solution)/shard_map/ppermute | solution.py:21
  45.4 1.7 %collective-permute-start.15 = (bf16[64,512]{1,0:T(8,128)(2,1)S(1)}, bf16[64,512]{1,0:T(8,128)(2,1)S(1)}, u32[]{:S(2)}, u32[]{:S(2)}) collective-permute-start(bf16[64,512]{1,0:T(8,128)(2,1)S(1)} %shard_map.125.refs_0_), channel_id=1, source_target_pairs={{0,12},{4,0},{8,4},{12,8},{1,13},{5,1},{9,5},{13,9},{2,14},{6,2},{... | collective-permute-start | bytes 196616 | tf_op jit(solution)/shard_map/ppermute | solution.py:21
  47.8 1.3 %collective-permute-start.19 = (f32[32,896]{1,0:T(8,128)S(1)}, f32[32,896]{1,0:T(8,128)S(1)}, u32[]{:S(2)}, u32[]{:S(2)}) collective-permute-start(f32[32,896]{1,0:T(8,128)S(1)} %get-tuple-element.38), channel_id=1, source_target_pairs={{0,2},{1,3},{2,0},{3,1},{4,6},{5,7},{6,4},{7,5},{8,10},{9,11},{10,... | collective-permute-start | bytes 344072 | tf_op jit(solution)/shard_map/ppermute | solution.py:387
  50.0 1.9 %collective-permute-done.14.refs_2_ = bf16[64,512]{1,0:T(8,128)(2,1)S(1)} collective-permute-done((bf16[64,512]{1,0:T(8,128)(2,1)S(1)}, bf16[64,512]{1,0:T(8,128)(2,1)S(1)}, u32[]{:S(2)}, u32[]{:S(2)}) %collective-permute-start.14) | collective-permute-done | bytes 65568 | tf_op jit(solution)/shard_map/ppermute | solution.py:21
  54.0 1.3 %collective-permute-start.21 = (bf16[8,896]{1,0:T(8,128)(2,1)S(1)}, bf16[8,896]{1,0:T(8,128)(2,1)S(1)}, u32[]{:S(2)}, u32[]{:S(2)}) collective-permute-start(bf16[8,896]{1,0:T(8,128)(2,1)S(1)} %get-tuple-element.39), channel_id=1, source_target_pairs={{0,2},{2,0},{4,6},{6,4},{8,10},{10,8},{12,14},{14,12},{1,3},{3,1},... | collective-permute-start | bytes 43016 | tf_op jit(solution)/shard_map/ppermute | solution.py:382
  55.3 1.5 %collective-permute-start.22 = (bf16[8,896]{1,0:T(8,128)(2,1)S(1)}, bf16[8,896]{1,0:T(8,128)(2,1)S(1)}, u32[]{:S(2)}, u32[]{:S(2)}) collective-permute-start(bf16[8,896]{1,0:T(8,128)(2,1)S(1)} %get-tuple-element.40), channel_id=1, source_target_pairs={{0,6},{2,4},{4,10},{6,8},{8,14},{10,12},{12,2},{14,0},{1,7},{3,5},... | collective-permute-start | bytes 43016 | tf_op jit(solution)/shard_map/ppermute | solution.py:382
  56.8 2.0 %collective-permute-start.23 = (bf16[8,896]{1,0:T(8,128)(2,1)S(1)}, bf16[8,896]{1,0:T(8,128)(2,1)S(1)}, u32[]{:S(2)}, u32[]{:S(2)}) collective-permute-start(bf16[8,896]{1,0:T(8,128)(2,1)S(1)} %get-tuple-element.41), channel_id=1, source_target_pairs={{0,10},{2,8},{4,14},{6,12},{8,2},{10,0},{12,6},{14,4},{1,11},{3,9}... | collective-permute-start | bytes 43016 | tf_op jit(solution)/shard_map/ppermute | solution.py:382
  58.8 2.0 %collective-permute-start.24 = (bf16[8,896]{1,0:T(8,128)(2,1)S(1)}, bf16[8,896]{1,0:T(8,128)(2,1)S(1)}, u32[]{:S(2)}, u32[]{:S(2)}) collective-permute-start(bf16[8,896]{1,0:T(8,128)(2,1)S(1)} %get-tuple-element.42), channel_id=1, source_target_pairs={{0,14},{2,12},{4,2},{6,0},{8,6},{10,4},{12,10},{14,8},{1,15},{3,13... | collective-permute-start | bytes 43016 | tf_op jit(solution)/shard_map/ppermute | solution.py:382
  (63 shorter events, 14.3 us)
Async XLA Ops:
  1.0 9.0 %collective-permute-start = (bf16[32,1600]{1,0:T(8,128)(2,1)S(1)}, bf16[32,1600]{1,0:T(8,128)(2,1)S(1)}, u32[]{:S(2)}, u32[]{:S(2)}) collective-permute-start(bf16[32,1600]{1,0:T(8,128)(2,1)S(1)} %get-tuple-element.25), channel_id=1, source_target_pairs={{0,4},{4,8},{8,12},{12,0},{1,5},{5,9},{9,13},{13,1},{2,6},{6,10},{... | collective-permute-start | bytes 307208 | tf_op jit(solution)/shard_map/ppermute | solution.py:21
  4.1 9.7 %collective-permute-start.1 = (bf16[32,1600]{1,0:T(8,128)(2,1)S(1)}, bf16[32,1600]{1,0:T(8,128)(2,1)S(1)}, u32[]{:S(2)}, u32[]{:S(2)}) collective-permute-start(bf16[32,1600]{1,0:T(8,128)(2,1)S(1)} %get-tuple-element.26), channel_id=1, source_target_pairs={{0,8},{4,12},{8,0},{12,4},{1,9},{5,13},{9,1},{13,5},{2,10},{6,14},... | collective-permute-start | bytes 307208 | tf_op jit(solution)/shard_map/ppermute | solution.py:21
  6.7 7.1 %collective-permute-start.2 = (bf16[32,1600]{1,0:T(8,128)(2,1)S(1)}, bf16[32,1600]{1,0:T(8,128)(2,1)S(1)}, u32[]{:S(2)}, u32[]{:S(2)}) collective-permute-start(bf16[32,1600]{1,0:T(8,128)(2,1)S(1)} %get-tuple-element.27), channel_id=1, source_target_pairs={{0,12},{4,0},{8,4},{12,8},{1,13},{5,1},{9,5},{13,9},{2,14},{6,2},{... | collective-permute-start | bytes 307208 | tf_op jit(solution)/shard_map/ppermute | solution.py:21
  15.0 1.9 %collective-permute-start.3 = (bf16[32,896]{1,0:T(8,128)(2,1)S(1)}, bf16[32,896]{1,0:T(8,128)(2,1)S(1)}, u32[]{:S(2)}, u32[]{:S(2)}) collective-permute-start(bf16[32,896]{1,0:T(8,128)(2,1)S(1)} %get-tuple-element.29), channel_id=1, source_target_pairs={{0,1},{1,0},{2,3},{3,2},{4,5},{5,4},{6,7},{7,6},{8,9},{9,8},{10,11... | collective-permute-start | bytes 172040 | tf_op jit(solution)/shard_map/ppermute | solution.py:387
  15.0 4.3 %collective-permute-start.4 = (bf16[32,896]{1,0:T(8,128)(2,1)S(1)}, bf16[32,896]{1,0:T(8,128)(2,1)S(1)}, u32[]{:S(2)}, u32[]{:S(2)}) collective-permute-start(bf16[32,896]{1,0:T(8,128)(2,1)S(1)} %get-tuple-element.30), channel_id=1, source_target_pairs={{0,2},{1,3},{2,0},{3,1},{4,6},{5,7},{6,4},{7,5},{8,10},{9,11},{10,... | collective-permute-start | bytes 172040 | tf_op jit(solution)/shard_map/ppermute | solution.py:387
  16.6 3.9 %collective-permute-start.5 = (bf16[32,896]{1,0:T(8,128)(2,1)S(1)}, bf16[32,896]{1,0:T(8,128)(2,1)S(1)}, u32[]{:S(2)}, u32[]{:S(2)}) collective-permute-start(bf16[32,896]{1,0:T(8,128)(2,1)S(1)} %get-tuple-element.31), channel_id=1, source_target_pairs={{0,3},{1,2},{2,1},{3,0},{4,7},{5,6},{6,5},{7,4},{8,11},{9,10},{10,... | collective-permute-start | bytes 172040 | tf_op jit(solution)/shard_map/ppermute | solution.py:387
  20.5 6.2 %collective-permute-start.6 = (bf16[32,896]{1,0:T(8,128)(2,1)S(1)}, bf16[32,896]{1,0:T(8,128)(2,1)S(1)}, u32[]{:S(2)}, u32[]{:S(2)}) collective-permute-start(bf16[32,896]{1,0:T(8,128)(2,1)S(1)} %get-tuple-element.32.refs_0_), channel_id=1, source_target_pairs={{0,4},{4,8},{8,12},{12,0},{1,5},{5,9},{9,13},{13,1},{2,6},{6,10},{... | collective-permute-start | bytes 172040 | tf_op jit(solution)/shard_map/ppermute | solution.py:21
  23.3 5.8 %collective-permute-start.7 = (bf16[32,896]{1,0:T(8,128)(2,1)S(1)}, bf16[32,896]{1,0:T(8,128)(2,1)S(1)}, u32[]{:S(2)}, u32[]{:S(2)}) collective-permute-start(bf16[32,896]{1,0:T(8,128)(2,1)S(1)} %get-tuple-element.32.refs_0_), channel_id=1, source_target_pairs={{0,8},{4,12},{8,0},{12,4},{1,9},{5,13},{9,1},{13,5},{2,10},{6,14},... | collective-permute-start | bytes 172040 | tf_op jit(solution)/shard_map/ppermute | solution.py:21
  24.9 4.8 %collective-permute-start.8 = (bf16[32,896]{1,0:T(8,128)(2,1)S(1)}, bf16[32,896]{1,0:T(8,128)(2,1)S(1)}, u32[]{:S(2)}, u32[]{:S(2)}) collective-permute-start(bf16[32,896]{1,0:T(8,128)(2,1)S(1)} %get-tuple-element.32.refs_0_), channel_id=1, source_target_pairs={{0,12},{4,0},{8,4},{12,8},{1,13},{5,1},{9,5},{13,9},{2,14},{6,2},{... | collective-permute-start | bytes 172040 | tf_op jit(solution)/shard_map/ppermute | solution.py:21
  29.9 1.6 %collective-permute-start.10 = (bf16[32,3712]{1,0:T(8,128)(2,1)S(1)}, bf16[32,3712]{1,0:T(8,128)(2,1)S(1)}, u32[]{:S(2)}, u32[]{:S(2)}) collective-permute-start(bf16[32,3712]{1,0:T(8,128)(2,1)S(1)} %shard_map.122.near.refs_5_), channel_id=1, source_target_pairs={{0,1},{1,0},{2,3},{3,2},{4,5},{5,4},{6,7},{7,6},{8,9},{9,8},{10,11... | collective-permute-start | bytes 712712 | tf_op jit(solution)/shard_map/ppermute | solution.py:387
  29.9 8.2 %collective-permute-start.9 = (bf16[32,3712]{1,0:T(8,128)(2,1)S(1)}, bf16[32,3712]{1,0:T(8,128)(2,1)S(1)}, u32[]{:S(2)}, u32[]{:S(2)}) collective-permute-start(bf16[32,3712]{1,0:T(8,128)(2,1)S(1)} %shard_map.122.near.refs_5_), channel_id=1, source_target_pairs={{0,2},{1,3},{2,0},{3,1},{4,6},{5,7},{6,4},{7,5},{8,10},{9,11},{10,... | collective-permute-start | bytes 712712 | tf_op jit(solution)/shard_map/ppermute | solution.py:387
  32.8 6.1 %collective-permute-start.11 = (bf16[64,512]{1,0:T(8,128)(2,1)S(1)}, bf16[64,512]{1,0:T(8,128)(2,1)S(1)}, u32[]{:S(2)}, u32[]{:S(2)}) collective-permute-start(bf16[64,512]{1,0:T(8,128)(2,1)S(1)} %shard_map.123.refs_0_), channel_id=1, source_target_pairs={{0,4},{4,8},{8,12},{12,0},{1,5},{5,9},{9,13},{13,1},{2,6},{6,10},{... | collective-permute-start | bytes 196616 | tf_op jit(solution)/shard_map/ppermute | solution.py:21
  38.9 2.9 %collective-permute-start.12 = (bf16[32,3712]{1,0:T(8,128)(2,1)S(1)}, bf16[32,3712]{1,0:T(8,128)(2,1)S(1)}, u32[]{:S(2)}, u32[]{:S(2)}) collective-permute-start(bf16[32,3712]{1,0:T(8,128)(2,1)S(1)} %shard_map.124.near.refs_5_), channel_id=1, source_target_pairs={{0,1},{1,0},{2,3},{3,2},{4,5},{5,4},{6,7},{7,6},{8,9},{9,8},{10,11... | collective-permute-start | bytes 712712 | tf_op jit(solution)/shard_map/ppermute | solution.py:387
  38.9 8.2 %collective-permute-start.16 = (bf16[64,512]{1,0:T(8,128)(2,1)S(1)}, bf16[64,512]{1,0:T(8,128)(2,1)S(1)}, u32[]{:S(2)}, u32[]{:S(2)}) collective-permute-start(bf16[64,512]{1,0:T(8,128)(2,1)S(1)} %shard_map.123.refs_0_), channel_id=1, source_target_pairs={{0,8},{4,12},{8,0},{12,4},{1,9},{5,13},{9,1},{13,5},{2,10},{6,14},... | collective-permute-start | bytes 196616 | tf_op jit(solution)/shard_map/ppermute | solution.py:21
  39.0 8.1 %collective-permute-start.17 = (bf16[64,512]{1,0:T(8,128)(2,1)S(1)}, bf16[64,512]{1,0:T(8,128)(2,1)S(1)}, u32[]{:S(2)}, u32[]{:S(2)}) collective-permute-start(bf16[64,512]{1,0:T(8,128)(2,1)S(1)} %shard_map.123.refs_0_), channel_id=1, source_target_pairs={{0,12},{4,0},{8,4},{12,8},{1,13},{5,1},{9,5},{13,9},{2,14},{6,2},{... | collective-permute-start | bytes 196616 | tf_op jit(solution)/shard_map/ppermute | solution.py:21
  43.2 6.8 %collective-permute-start.13 = (bf16[64,512]{1,0:T(8,128)(2,1)S(1)}, bf16[64,512]{1,0:T(8,128)(2,1)S(1)}, u32[]{:S(2)}, u32[]{:S(2)}) collective-permute-start(bf16[64,512]{1,0:T(8,128)(2,1)S(1)} %shard_map.125.refs_0_), channel_id=1, source_target_pairs={{0,4},{4,8},{8,12},{12,0},{1,5},{5,9},{9,13},{13,1},{2,6},{6,10},{... | collective-permute-start | bytes 196616 | tf_op jit(solution)/shard_map/ppermute | solution.py:21
  43.3 8.6 %collective-permute-start.14 = (bf16[64,512]{1,0:T(8,128)(2,1)S(1)}, bf16[64,512]{1,0:T(8,128)(2,1)S(1)}, u32[]{:S(2)}, u32[]{:S(2)}) collective-permute-start(bf16[64,512]{1,0:T(8,128)(2,1)S(1)} %shard_map.125.refs_0_), channel_id=1, source_target_pairs={{0,8},{4,12},{8,0},{12,4},{1,9},{5,13},{9,1},{13,5},{2,10},{6,14},... | collective-permute-start | bytes 196616 | tf_op jit(solution)/shard_map/ppermute | solution.py:21
  45.4 6.5 %collective-permute-start.15 = (bf16[64,512]{1,0:T(8,128)(2,1)S(1)}, bf16[64,512]{1,0:T(8,128)(2,1)S(1)}, u32[]{:S(2)}, u32[]{:S(2)}) collective-permute-start(bf16[64,512]{1,0:T(8,128)(2,1)S(1)} %shard_map.125.refs_0_), channel_id=1, source_target_pairs={{0,12},{4,0},{8,4},{12,8},{1,13},{5,1},{9,5},{13,9},{2,14},{6,2},{... | collective-permute-start | bytes 196616 | tf_op jit(solution)/shard_map/ppermute | solution.py:21
  47.8 5.5 %collective-permute-start.19 = (f32[32,896]{1,0:T(8,128)S(1)}, f32[32,896]{1,0:T(8,128)S(1)}, u32[]{:S(2)}, u32[]{:S(2)}) collective-permute-start(f32[32,896]{1,0:T(8,128)S(1)} %get-tuple-element.38), channel_id=1, source_target_pairs={{0,2},{1,3},{2,0},{3,1},{4,6},{5,7},{6,4},{7,5},{8,10},{9,11},{10,... | collective-permute-start | bytes 344072 | tf_op jit(solution)/shard_map/ppermute | solution.py:387
  49.2 4.2 %collective-permute-start.20 = (bf16[32,896]{1,0:T(8,128)(2,1)S(1)}, bf16[32,896]{1,0:T(8,128)(2,1)S(1)}, u32[]{:S(2)}, u32[]{:S(2)}) collective-permute-start(bf16[32,896]{1,0:T(8,128)(2,1)S(1)} %get-tuple-element.35.refs_7_), channel_id=1, source_target_pairs={{0,3},{1,2},{2,1},{3,0},{4,7},{5,6},{6,5},{7,4},{8,11},{9,10},{10,... | collective-permute-start | bytes 172040 | tf_op jit(solution)/shard_map/ppermute | solution.py:387
  54.0 6.8 %collective-permute-start.21 = (bf16[8,896]{1,0:T(8,128)(2,1)S(1)}, bf16[8,896]{1,0:T(8,128)(2,1)S(1)}, u32[]{:S(2)}, u32[]{:S(2)}) collective-permute-start(bf16[8,896]{1,0:T(8,128)(2,1)S(1)} %get-tuple-element.39), channel_id=1, source_target_pairs={{0,2},{2,0},{4,6},{6,4},{8,10},{10,8},{12,14},{14,12},{1,3},{3,1},... | collective-permute-start | bytes 43016 | tf_op jit(solution)/shard_map/ppermute | solution.py:382
  55.3 6.4 %collective-permute-start.22 = (bf16[8,896]{1,0:T(8,128)(2,1)S(1)}, bf16[8,896]{1,0:T(8,128)(2,1)S(1)}, u32[]{:S(2)}, u32[]{:S(2)}) collective-permute-start(bf16[8,896]{1,0:T(8,128)(2,1)S(1)} %get-tuple-element.40), channel_id=1, source_target_pairs={{0,6},{2,4},{4,10},{6,8},{8,14},{10,12},{12,2},{14,0},{1,7},{3,5},... | collective-permute-start | bytes 43016 | tf_op jit(solution)/shard_map/ppermute | solution.py:382
  56.8 5.5 %collective-permute-start.23 = (bf16[8,896]{1,0:T(8,128)(2,1)S(1)}, bf16[8,896]{1,0:T(8,128)(2,1)S(1)}, u32[]{:S(2)}, u32[]{:S(2)}) collective-permute-start(bf16[8,896]{1,0:T(8,128)(2,1)S(1)} %get-tuple-element.41), channel_id=1, source_target_pairs={{0,10},{2,8},{4,14},{6,12},{8,2},{10,0},{12,6},{14,4},{1,11},{3,9}... | collective-permute-start | bytes 43016 | tf_op jit(solution)/shard_map/ppermute | solution.py:382
  58.8 4.6 %collective-permute-start.24 = (bf16[8,896]{1,0:T(8,128)(2,1)S(1)}, bf16[8,896]{1,0:T(8,128)(2,1)S(1)}, u32[]{:S(2)}, u32[]{:S(2)}) collective-permute-start(bf16[8,896]{1,0:T(8,128)(2,1)S(1)} %get-tuple-element.42), channel_id=1, source_target_pairs={{0,14},{2,12},{4,2},{6,0},{8,6},{10,4},{12,10},{14,8},{1,15},{3,13... | collective-permute-start | bytes 43016 | tf_op jit(solution)/shard_map/ppermute | solution.py:382
  (13 other events, 138.0 us)
